TPU v7x, 32 devices: a whole 2x2x4 slice. The times are simulated.
32 devices in a mesh: fsdp: 2 (over x), context: 4 (over z), tensor: 4 (over y, core).
Axes of the slice: x: 2, y: 2, z: 4, core: 2. Of those that a mesh axis runs over, the one named last changes fastest.
Arguments:
- residual_in: bfloat16 [2, 1024, 1536], P('fsdp', 'context'), may hold values from -12 to 12
- token_mask: int32 [2, 1024], P('fsdp'), may hold values from 0 to 1, as said below
- parent_blocks: int32 [2, 8], P('fsdp'), may hold values from 0 to 6, as said below
- expert_routes: int32 [2, 1024, 8], P('fsdp', 'context'), may hold values from 0 to 15, all different within a row; in each aligned block of 256 rows (0 to 255, 256 to 511, ..., all dimensions but the last counted through in order) at most 160 rows name the same one
- attn_gain: bfloat16 [1536], P('fsdp'), may hold values from 0.099609375 to 1.8984375
- query_weight: bfloat16 [1536, 1536], P('fsdp', 'tensor'), may hold values from -0.15625 to 0.15625
- key_weight: bfloat16 [1536, 512], P('fsdp', 'tensor'), may hold values from -0.15625 to 0.15625
- value_weight: bfloat16 [1536, 512], P('fsdp', 'tensor'), may hold values from -0.15625 to 0.15625
- output_weight: bfloat16 [1536, 1536], P('tensor', 'fsdp'), may hold values from -3 to 3
- ffn_gain: bfloat16 [1536], P('fsdp'), may hold values from 0.099609375 to 1.8984375
- router_weight: bfloat16 [1536, 16], P('fsdp'), may hold values from -0.078125 to 0.078125
- expert_weights: bfloat16 [16, 3, 1536, 512], P('fsdp', None, None, 'tensor'), may hold values from -2 to 2
- out_cotangent: float32 [2, 1024, 1536], P('fsdp', 'context'), may hold values from -6 to 6
Outputs:
- block_out: bfloat16 [2, 1024, 1536], P('fsdp', 'context')
- input_grad: float32 [2, 1024, 1536], P('fsdp', 'context')
- attn_gain_grad: float32 [1536], P('fsdp')
- query_grad: float32 [1536, 1536], P('fsdp', 'tensor')
- key_grad: float32 [1536, 512], P('fsdp', 'tensor')
- value_grad: float32 [1536, 512], P('fsdp', 'tensor')
- output_grad: float32 [1536, 1536], P('tensor', 'fsdp')
- ffn_gain_grad: float32 [1536], P('fsdp')
- router_grad: float32 [1536, 16], P('fsdp')
- expert_grad: float32 [16, 3, 1536, 512], P('fsdp', None, None, 'tensor')
- rms_stats: float32 [4], replicated
Inputs may be any that keep to these rules, and one draw needn't show every extreme that they name: `token_mask`: within each block of 128 positions the tokens with 1 come first and there is at least one; the first 4 blocks of every tree hold no padding. `parent_blocks`: block 0 gives 0, block b gives b - 1 for 0 < b < 4, every later block b gives a block from 3 to b - 1, and block 7 gives 6. `expert_routes`: each token names 8 different experts; among the 256 positions of one tree on one index of context no expert is named more than 160 times, a bound that some block reaches in some of these aligned blocks.
All inputs are finite; a program needn't handle non-finite values.
Results may differ from a plain program's by a relative error of at most 0.015.
The roundings to bfloat16 on the way count: a program that leaves them out, or rounds other values in their place, can miss the bound.
Values may be sent and summed in bfloat16 or wider, within the bound.
A program may use at most 256 MiB of HBM per device.

v0:
```python
import jax
import jax.numpy as jnp
from jax import lax
from jax.sharding import PartitionSpec as P

HEAD_DIM = 64
TOPK = 8
EXPERTS = 16
CAP = 160
SEG = 128


EPS = 1e-06


def ancestry(parents):
    blocks = parents.shape[-1]
    diagonal = jnp.eye(blocks, dtype=jnp.int32)
    upward = (parents[..., :, None] == jnp.arange(blocks, dtype=jnp.int32)).astype(jnp.int32)
    closure = jnp.minimum(diagonal + upward, 1)
    for squaring in range(blocks.bit_length()):
        closure = jnp.minimum(jnp.matmul(closure, closure), 1)
    return closure


def rotary(values, angles):
    half_dim = values.shape[-1] // 2
    rotated = jnp.concatenate([-values[..., half_dim:], values[..., :half_dim]], -1)
    return values * jnp.cos(angles) + rotated * jnp.sin(angles)


def rms_normalize(values, gains):
    return values * lax.rsqrt(jnp.mean(values * values, -1, keepdims=True) + EPS) * gains


def gated_unit(gate_vals, up_vals):
    return jax.nn.silu(gate_vals) * up_vals


def per_device(
    residual_in,
    token_mask,
    parent_blocks,
    expert_routes,
    attn_gain,
    query_weight,
    key_weight,
    value_weight,
    output_weight,
    ffn_gain,
    router_weight,
    expert_weights,
    out_cotangent,
):
    tree_count, local_len, model_width = residual_in.shape
    tree_len = token_mask.shape[1]
    rows_count = tree_count * local_len
    context_index = lax.axis_index("context")
    gain_one, gain_two, w_query, w_key, w_value, w_output, w_router = (
        lax.all_gather(attn_gain, "fsdp", axis=0, tiled=True),
        lax.all_gather(ffn_gain, "fsdp", axis=0, tiled=True),
        lax.all_gather(query_weight, "fsdp", axis=0, tiled=True),
        lax.all_gather(key_weight, "fsdp", axis=0, tiled=True),
        lax.all_gather(value_weight, "fsdp", axis=0, tiled=True),
        lax.all_gather(output_weight, "fsdp", axis=1, tiled=True),
        lax.all_gather(router_weight, "fsdp", axis=0, tiled=True),
    )
    w_experts = lax.all_gather(expert_weights, "fsdp", axis=0, tiled=True)
    gain_one = gain_one.astype(jnp.float32)
    gain_two = gain_two.astype(jnp.float32)
    heads_local = w_query.shape[1] // HEAD_DIM
    kv_local = w_key.shape[1] // HEAD_DIM
    group_size = heads_local // kv_local
    positions = context_index * local_len + jnp.arange(local_len, dtype=jnp.int32)
    blocks_total = parent_blocks.shape[1]
    pick_block = (
        positions[:, None] // SEG == jnp.arange(blocks_total, dtype=jnp.int32)[None, :]
    ).astype(jnp.int32)
    closure = ancestry(parent_blocks)
    row_reach = jnp.matmul(pick_block, closure)
    block_depth = jnp.sum(closure, -1) - 1
    token_depth = jnp.matmul(block_depth, pick_block.T)
    rope_pos = (token_depth * SEG + positions[None, :] % SEG).astype(jnp.float32)
    half_freq = 10000.0 ** (-(jnp.arange(HEAD_DIM // 2, dtype=jnp.float32) * 2.0) / HEAD_DIM)
    frequencies = jnp.concatenate([half_freq, half_freq])
    angles = rope_pos[:, :, None, None] * frequencies
    key_pos = jnp.arange(tree_len, dtype=jnp.int32)
    allowed = (
        (jnp.repeat(row_reach, SEG, axis=2) > 0)
        & (key_pos[None, None, :] <= positions[None, :, None])
        & (token_mask[:, None, :] > 0)
    )
    visible = allowed[:, None, None]
    stream = residual_in.astype(jnp.float32)
    normed_one = rms_normalize(stream, gain_one).astype(jnp.bfloat16)
    queries = jnp.einsum("tld,dc->tlc", normed_one, w_query, preferred_element_type=jnp.float32)
    keys_raw = jnp.einsum("tld,dc->tlc", normed_one, w_key, preferred_element_type=jnp.float32)
    values_raw = jnp.einsum("tld,dc->tlc", normed_one, w_value, preferred_element_type=jnp.float32)
    query_heads = queries.reshape(tree_count, local_len, heads_local, HEAD_DIM)
    key_heads = keys_raw.reshape(tree_count, local_len, kv_local, HEAD_DIM)
    query_rot = (
        rotary(query_heads, angles)
        .astype(jnp.bfloat16)
        .reshape(tree_count, local_len, kv_local, group_size, HEAD_DIM)
    )
    key_rot = (
        rotary(key_heads, angles)
        .astype(jnp.bfloat16)
        .reshape(tree_count, local_len, kv_local * HEAD_DIM)
    )
    value_low = values_raw.astype(jnp.bfloat16)
    keys_all, values_all = (
        lax.all_gather(key_rot, "context", axis=1, tiled=True),
        lax.all_gather(value_low, "context", axis=1, tiled=True),
    )
    keys_all = keys_all.reshape(tree_count, tree_len, kv_local, HEAD_DIM)
    values_all = values_all.reshape(tree_count, tree_len, kv_local, HEAD_DIM)
    scores = (
        jnp.einsum("tlkgh,tmkh->tkglm", query_rot, keys_all, preferred_element_type=jnp.float32)
        * 0.125
    )
    masked = jnp.where(visible, scores, -jnp.inf)
    row_peak = jnp.max(masked, -1, keepdims=True)
    log_total = row_peak + jnp.log(jnp.sum(jnp.exp(masked - row_peak), -1, keepdims=True))
    attn_probs = jnp.exp(masked - log_total).astype(jnp.bfloat16)
    attended = jnp.einsum(
        "tkglm,tmkh->tlkgh", attn_probs, values_all, preferred_element_type=jnp.float32
    )
    attended_low = attended.reshape(tree_count, local_len, heads_local * HEAD_DIM).astype(
        jnp.bfloat16
    )
    attn_part = jnp.einsum(
        "tlc,cd->tld", attended_low, w_output, preferred_element_type=jnp.float32
    )
    attn_out = lax.psum(attn_part, "tensor")
    middle = stream + attn_out
    normed_two = rms_normalize(middle, gain_two).astype(jnp.bfloat16)
    router_logits = jnp.einsum(
        "tld,de->tle", normed_two, w_router, preferred_element_type=jnp.float32
    )
    router_probs = jax.nn.softmax(router_logits, -1)
    route_hot = (expert_routes[..., None] == jnp.arange(EXPERTS, dtype=jnp.int32)).astype(
        jnp.float32
    )
    gate_probs = jnp.sum(route_hot * router_probs[:, :, None, :], -1)
    flat_routes = expert_routes.reshape(tree_count, local_len * TOPK)
    hot_int = (flat_routes[..., None] == jnp.arange(EXPERTS, dtype=jnp.int32)).astype(jnp.int32)
    slot_rank = jnp.sum((jnp.cumsum(hot_int, 1) - 1) * hot_int, -1)
    tree_ids = jnp.arange(tree_count, dtype=jnp.int32)[:, None]
    slot_index = ((flat_routes * tree_count + tree_ids) * CAP + slot_rank).reshape(-1)
    row_token = (
        tree_ids * local_len + jnp.arange(local_len * TOPK, dtype=jnp.int32)[None, :] // TOPK
    ).reshape(-1)
    slot_width = tree_count * CAP
    token_of_slot = (
        jnp.full((EXPERTS * slot_width,), rows_count, jnp.int32)
        .at[slot_index]
        .set(row_token)
        .reshape(EXPERTS, slot_width)
    )
    gate_of_slot = (
        jnp.zeros((EXPERTS * slot_width,), jnp.float32)
        .at[slot_index]
        .set(gate_probs.reshape(-1))
        .reshape(EXPERTS, slot_width)
    )
    padded_two = jnp.concatenate(
        [normed_two.reshape(rows_count, model_width), jnp.zeros((1, model_width), jnp.bfloat16)], 0
    )
    expert_rows = padded_two[token_of_slot]
    padded_cot = jnp.concatenate(
        [out_cotangent.reshape(rows_count, model_width), jnp.zeros((1, model_width), jnp.float32)],
        0,
    )

    def expert_forward(running, operands):
        rows_in, weights, slot_tokens, slot_gates = operands
        gate_up = jnp.einsum(
            "rd,sdf->srf", rows_in, weights[:2], preferred_element_type=jnp.float32
        )
        hidden = gated_unit(gate_up[0], gate_up[1]).astype(jnp.bfloat16)
        produced = jnp.einsum("rf,df->rd", hidden, weights[2], preferred_element_type=jnp.float32)
        running = running.at[slot_tokens].add(slot_gates[:, None] * produced)
        gate_grad = jnp.sum(produced * padded_cot[slot_tokens], -1)
        return (running, (gate_up, gate_grad))

    ffn_part, (gate_up_all, gate_grad_slot) = lax.scan(
        expert_forward,
        jnp.zeros((rows_count + 1, model_width), jnp.float32),
        (expert_rows, w_experts, token_of_slot, gate_of_slot),
    )
    gate_grad_rows = gate_grad_slot.reshape(-1)[slot_index].reshape(tree_count, local_len, TOPK)
    ffn_out, gate_grad = lax.psum(
        (ffn_part[:rows_count].reshape(tree_count, local_len, model_width), gate_grad_rows),
        "tensor",
    )
    block_out = middle + ffn_out
    own_mask = lax.dynamic_slice_in_dim(token_mask, context_index * local_len, local_len, 1).astype(
        jnp.float32
    )
    square_sums = jnp.stack(
        [
            jnp.sum(jnp.sum(component * component, -1) * own_mask)
            for component in (stream, attn_out, middle, ffn_out)
        ]
    )
    square_totals, valid_total = lax.psum((square_sums, jnp.sum(own_mask)), ("fsdp", "context"))
    rms_stats = jnp.sqrt(square_totals / (valid_total * model_width))
    w_back = lax.all_gather(expert_weights, "fsdp", axis=0, tiled=True)

    def expert_backward(running, operands):
        weights, slot_tokens, slot_gates, gate_up = operands
        down_grad = (slot_gates[:, None] * padded_cot[slot_tokens]).astype(jnp.bfloat16)
        hidden_grad = jnp.einsum(
            "rd,df->rf", down_grad, weights[2], preferred_element_type=jnp.float32
        )
        hidden_val, pullback = jax.vjp(gated_unit, gate_up[0], gate_up[1])
        gate_diff, up_diff = pullback(hidden_grad)
        gate_up_grad = jnp.stack([gate_diff, up_diff]).astype(jnp.bfloat16)
        rows_grad = jnp.einsum(
            "srf,sdf->rd", gate_up_grad, weights[:2], preferred_element_type=jnp.float32
        )
        running = running.at[slot_tokens].add(rows_grad)
        return (running, (gate_up_grad, hidden_val.astype(jnp.bfloat16), down_grad))

    normed_part, (gate_up_grads, hidden_all, down_grads) = lax.scan(
        expert_backward,
        jnp.zeros((rows_count + 1, model_width), jnp.float32),
        (w_back, token_of_slot, gate_of_slot, gate_up_all),
    )
    expert_normed_grad = lax.psum(
        normed_part[:rows_count].reshape(tree_count, local_len, model_width), "tensor"
    )
    rows_in = expert_rows
    gate_terms = jnp.einsum(
        "erd,esrf->esdf", rows_in, gate_up_grads, preferred_element_type=jnp.float32
    )
    down_terms = jnp.einsum(
        "erd,erf->edf", down_grads, hidden_all, preferred_element_type=jnp.float32
    )
    expert_grad_part = lax.psum_scatter(
        jnp.concatenate([gate_terms, down_terms[:, None]], 1),
        "fsdp",
        scatter_dimension=0,
        tiled=True,
    )
    prob_grad = jnp.sum(gate_grad[..., None] * route_hot, 2)
    logit_grad = (
        router_probs * (prob_grad - jnp.sum(router_probs * prob_grad, -1, keepdims=True))
    ).astype(jnp.bfloat16)
    normed_two_grad = expert_normed_grad + jnp.einsum(
        "tle,de->tld", logit_grad, w_router, preferred_element_type=jnp.float32
    )
    router_grad_full = jnp.einsum(
        "tld,tle->de", normed_two, logit_grad, preferred_element_type=jnp.float32
    )
    middle_norm_grad, ffn_gain_full = jax.vjp(rms_normalize, middle, gain_two)[1](normed_two_grad)
    middle_grad = out_cotangent + middle_norm_grad
    attn_cot = middle_grad.astype(jnp.bfloat16)
    output_grad_full = jnp.einsum(
        "tlc,tld->cd", attended_low, attn_cot, preferred_element_type=jnp.float32
    )
    attended_grad = jnp.einsum(
        "tld,cd->tlc", attn_cot, w_output, preferred_element_type=jnp.float32
    ).astype(jnp.bfloat16)
    attended_grad = attended_grad.reshape(tree_count, local_len, kv_local, group_size, HEAD_DIM)
    scores_again = (
        jnp.einsum("tlkgh,tmkh->tkglm", query_rot, keys_all, preferred_element_type=jnp.float32)
        * 0.125
    )
    exact_probs = jnp.exp(jnp.where(visible, scores_again, -jnp.inf) - log_total)
    prob_grad_attn = jnp.einsum(
        "tlkgh,tmkh->tkglm", attended_grad, values_all, preferred_element_type=jnp.float32
    )
    row_delta = jnp.sum(exact_probs * prob_grad_attn, -1, keepdims=True)
    score_grad = (exact_probs * (prob_grad_attn - row_delta)).astype(jnp.bfloat16)
    query_rot_grad = (
        jnp.einsum("tkglm,tmkh->tlkgh", score_grad, keys_all, preferred_element_type=jnp.float32)
        * 0.125
    )
    key_grad_all = (
        jnp.einsum("tkglm,tlkgh->tmkh", score_grad, query_rot, preferred_element_type=jnp.float32)
        * 0.125
    )
    value_grad_all = jnp.einsum(
        "tkglm,tlkgh->tmkh",
        exact_probs.astype(jnp.bfloat16),
        attended_grad,
        preferred_element_type=jnp.float32,
    )
    key_rot_grad, value_grad_sum = (
        lax.psum_scatter(
            key_grad_all.reshape(tree_count, tree_len, kv_local * HEAD_DIM),
            "context",
            scatter_dimension=1,
            tiled=True,
        ),
        lax.psum_scatter(
            value_grad_all.reshape(tree_count, tree_len, kv_local * HEAD_DIM),
            "context",
            scatter_dimension=1,
            tiled=True,
        ),
    )

    def rotate_heads(raw_heads):
        return rotary(raw_heads, angles)

    query_low = jax.vjp(rotate_heads, query_heads)[1](
        query_rot_grad.reshape(tree_count, local_len, heads_local, HEAD_DIM)
    )[0]
    query_low = query_low.astype(jnp.bfloat16).reshape(
        tree_count, local_len, heads_local * HEAD_DIM
    )
    key_low = jax.vjp(rotate_heads, key_heads)[1](
        key_rot_grad.reshape(tree_count, local_len, kv_local, HEAD_DIM)
    )[0]
    key_low = key_low.astype(jnp.bfloat16).reshape(tree_count, local_len, kv_local * HEAD_DIM)
    value_low_grad = value_grad_sum.astype(jnp.bfloat16)
    query_grad_full = jnp.einsum(
        "tld,tlc->dc", normed_one, query_low, preferred_element_type=jnp.float32
    )
    key_grad_full = jnp.einsum(
        "tld,tlc->dc", normed_one, key_low, preferred_element_type=jnp.float32
    )
    value_grad_full = jnp.einsum(
        "tld,tlc->dc", normed_one, value_low_grad, preferred_element_type=jnp.float32
    )
    normed_one_part = (
        jnp.einsum("tlc,dc->tld", query_low, w_query, preferred_element_type=jnp.float32)
        + jnp.einsum("tlc,dc->tld", key_low, w_key, preferred_element_type=jnp.float32)
        + jnp.einsum("tlc,dc->tld", value_low_grad, w_value, preferred_element_type=jnp.float32)
    )
    normed_one_grad = lax.psum(normed_one_part, "tensor")
    stream_norm_grad, attn_gain_full = jax.vjp(rms_normalize, stream, gain_one)[1](normed_one_grad)
    input_grad = middle_grad + stream_norm_grad
    gain_one_part, gain_two_part, query_part, key_part, value_part, output_part, router_part = (
        lax.psum_scatter(attn_gain_full, "fsdp", scatter_dimension=0, tiled=True),
        lax.psum_scatter(ffn_gain_full, "fsdp", scatter_dimension=0, tiled=True),
        lax.psum_scatter(query_grad_full, "fsdp", scatter_dimension=0, tiled=True),
        lax.psum_scatter(key_grad_full, "fsdp", scatter_dimension=0, tiled=True),
        lax.psum_scatter(value_grad_full, "fsdp", scatter_dimension=0, tiled=True),
        lax.psum_scatter(output_grad_full, "fsdp", scatter_dimension=1, tiled=True),
        lax.psum_scatter(router_grad_full, "fsdp", scatter_dimension=0, tiled=True),
    )
    (
        expert_piece,
        gain_one_piece,
        gain_two_piece,
        query_piece,
        key_piece,
        value_piece,
        output_piece,
        router_piece,
    ) = (
        lax.psum_scatter(expert_grad_part, "context", scatter_dimension=2, tiled=True),
        lax.psum_scatter(gain_one_part, "context", scatter_dimension=0, tiled=True),
        lax.psum_scatter(gain_two_part, "context", scatter_dimension=0, tiled=True),
        lax.psum_scatter(query_part, "context", scatter_dimension=0, tiled=True),
        lax.psum_scatter(key_part, "context", scatter_dimension=0, tiled=True),
        lax.psum_scatter(value_part, "context", scatter_dimension=0, tiled=True),
        lax.psum_scatter(output_part, "context", scatter_dimension=1, tiled=True),
        lax.psum_scatter(router_part, "context", scatter_dimension=0, tiled=True),
    )
    (
        expert_grad,
        attn_gain_grad,
        ffn_gain_grad,
        query_grad,
        key_grad,
        value_grad,
        output_grad,
        router_grad,
    ) = (
        lax.all_gather(expert_piece, "context", axis=2, tiled=True),
        lax.all_gather(gain_one_piece, "context", axis=0, tiled=True),
        lax.all_gather(gain_two_piece, "context", axis=0, tiled=True),
        lax.all_gather(query_piece, "context", axis=0, tiled=True),
        lax.all_gather(key_piece, "context", axis=0, tiled=True),
        lax.all_gather(value_piece, "context", axis=0, tiled=True),
        lax.all_gather(output_piece, "context", axis=1, tiled=True),
        lax.all_gather(router_piece, "context", axis=0, tiled=True),
    )
    return (
        block_out.astype(jnp.bfloat16),
        input_grad,
        attn_gain_grad,
        query_grad,
        key_grad,
        value_grad,
        output_grad,
        ffn_gain_grad,
        router_grad,
        expert_grad,
        rms_stats,
    )


def solution(mesh):
    return jax.shard_map(
        per_device,
        mesh=mesh,
        in_specs=(
            P("fsdp", "context", None),
            P("fsdp", None),
            P("fsdp", None),
            P("fsdp", "context", None),
            P("fsdp"),
            P("fsdp", "tensor"),
            P("fsdp", "tensor"),
            P("fsdp", "tensor"),
            P("tensor", "fsdp"),
            P("fsdp"),
            P("fsdp", None),
            P("fsdp", None, None, "tensor"),
            P("fsdp", "context", None),
        ),
        out_specs=(
            P("fsdp", "context", None),
            P("fsdp", "context", None),
            P("fsdp"),
            P("fsdp", "tensor"),
            P("fsdp", "tensor"),
            P("fsdp", "tensor"),
            P("tensor", "fsdp"),
            P("fsdp"),
            P("fsdp", None),
            P("fsdp", None, None, "tensor"),
            P(),
        ),
        check_vma=False,
    )
```

profile of v0, /device:TPU:0, one launch (start us, length us, event | category | flops | bytes accessed | tf_op | source)
XLA Modules:
  0.0 2382.9 jit_solution(1113790263971248075)
XLA Ops:
  24.9 14.6 all-gather.1
  48.7 13.8 all-gather
  100.9 17.7 all-reduce.21.cloned.1.call-done
  142.9 201.6 %all-gather.16.cloned.1.call-done = bf16[16,3,1536,128]{3,2,1,0:T(8,128)(2,1)} async-done(((bf16[8,3,1536,128]{3,2,1,0:T(8,128)(2,1)}), bf16[16,3,1536,128]{3,2,1,0:T(8,128)(2,1)}) %all-gather.16.cloned.1.call-update) | async-done | bytes 18874384 | tf_op jit(solution)/shard_map/all_gather | solution.py:68
  345.9 203.2 %while.30 = (s32[]{:T(128)}, f32[257,1536]{1,0:T(8,128)}, f32[16,2,160,128]{3,2,1,0:T(8,128)}, f32[16,160]{1,0:T(8,128)}, s32[16,160]{1,0:T(8,128)}, /*index=5*/...) while((s32[]{:T(128)}, f32[257,1536]{1,0:T(8,128)}, ...), condition=%wide.region_17.18_spmd, body=%wide.region_14.17_spmd.sunk | while | flops 189850944 | bytes 8669969 | solution.py:187
  549.2 245.1 %while.31 = (s32[]{:T(128)}, f32[257,1536]{1,0:T(8,128)S(1)}, bf16[16,2,160,128]{3,2,1,0:T(8,128)(2,1)}, bf16[16,160,128]{2,1,0:T(8,128)(2,1)}, bf16[16,160,1536...) while((s32[]{:T(128)}, f32[257,1536]{1,0:T(8,128)S(1)}, ...), condition=%wide.region_21.22_spmd, body=%wide.region_19.21_spmd.sunk | while | flops 190588384 | bytes 10490757 | solution.py:226
  808.4 14.1 psum.52
  822.7 16.7 all-reduce.23.cloned.1.call-done
  897.8 25.8 %pad_maximum_fusion = f32[16,3,1536,128]{2,3,1,0:T(8,128)} fusion(f32[16,1,1536,128]{2,3,1,0:T(8,128)} %convolution_bitcast_fusion.2, f32[16,2,1536,128]{2,3,1,0:T(8,128)} %convolution_bitcast_fusion.1), kind=kLoop, calls=%fused_computation.72 | loop fusion | flops 9437184 | bytes 75497472 | tf_op jit(solution)/shard_map/concatenate | solution.py:242
  941.3 34.4 %reduce-scatter.23.cloned.1.call-done = f32[768,384]{1,0:T(8,128)} async-done(((f32[1536,384]{1,0:T(8,128)}), f32[768,384]{1,0:T(8,128)}) %reduce-scatter.23.cloned.1.call-update) | async-done | bytes 1179664 | tf_op jit(solution)/shard_map/reduce_scatter | solution.py:340
  975.7 416.0 %reduce-scatter.39.cloned.1.call-done = f32[8,3,1536,128]{2,3,1,0:T(8,128)} async-done(((f32[16,3,1536,128]{2,3,1,0:T(8,128)}), f32[8,3,1536,128]{2,3,1,0:T(8,128)}) %reduce-scatter.39.cloned.1.call-update) | async-done | bytes 18874384 | tf_op jit(solution)/shard_map/reduce_scatter | solution.py:241
  1410.9 13.8 reduce-scatter.31.cloned.1.call-done
  1424.8 20.3 reduce-scatter.27.cloned.1.call-done
  1445.1 31.9 %reduce-scatter.43.cloned.1.call-done = f32[192,384]{1,0:T(8,128)} async-done(((f32[768,384]{1,0:T(8,128)}), f32[192,384]{1,0:T(8,128)}) %reduce-scatter.43.cloned.1.call-update) | async-done | bytes 294928
  1477.1 30.0 %reduce-scatter.25.cloned.1.call-done = f32[192,384]{1,0:T(8,128)} async-done(((f32[768,384]{1,0:T(8,128)}), f32[192,384]{1,0:T(8,128)}) %reduce-scatter.25.cloned.1.call-update) | async-done | bytes 294928 | tf_op jit(solution)/shard_map/reduce_scatter | solution.py:359
  1507.2 314.7 %reduce-scatter.41.cloned.1.call-done = f32[8,3,384,128]{2,3,1,0:T(8,128)} async-done(((f32[8,3,1536,128]{2,3,1,0:T(8,128)}), f32[8,3,384,128]{2,3,1,0:T(8,128)}) %reduce-scatter.41.cloned.1.call-update) | async-done | bytes 4718608 | tf_op jit(solution)/shard_map/reduce_scatter | solution.py:356
  1825.7 20.1 reduce-scatter.45.cloned.1.call-done
  1860.6 55.5 %all-reduce.25.cloned.1.call-done = (f32[1,256,1536]{2,1,0:T(8,128)}, f32[1,256,1536]{2,1,0:T(8,128)}) async-done(((f32[1,256,1536]{2,1,0:T(8,128)}, f32[1,256,1536]{2,1,0:T(8,128)}), (f32[1,256,1536]{2,1,0:T(8,128)}, f32[1,256,1536]{2,1,0:T(8,128)})) %all-reduce.25.cloned.1.call-update) | async-done | bytes 3145744 | tf_op jit(solution)/shard_map/psum | solution.py:193
  1922.7 22.1 all-reduce.12
  1978.4 18.1 all_gather.68
  1996.4 14.4 all_gather.67
  2013.5 17.9 all-gather.18.cloned.1.call-done
  2031.4 323.3 %all-gather.22.cloned.1.call-done = f32[8,3,1536,128]{2,3,1,0:T(8,128)} async-done(((f32[8,3,384,128]{2,3,1,0:T(8,128)}), f32[8,3,1536,128]{2,3,1,0:T(8,128)}) %all-gather.22.cloned.1.call-update) | async-done | bytes 18874384 | tf_op jit(solution)/shard_map/all_gather | solution.py:375
  2354.8 18.6 copy.87
  (727 shorter events, 708.6 us)
Async XLA Ops:
  7.2 55.7 %all-gather.12.cloned.1.call-start = ((), (), s32[]{:S(2)}) async-start(), calls=%async_computation.14 | async-start | bytes 1769472 | tf_op jit(solution)/shard_map/all_gather | solution.py:62
  7.9 62.6 %all-gather.14.cloned.1.call-start = ((), (), s32[]{:S(2)}) async-start(), calls=%async_computation.15 | async-start | bytes 1769472 | tf_op jit(solution)/shard_map/all_gather | solution.py:65
  8.7 109.9 %all-reduce.21.cloned.1.call-start = ((), (), s32[]{:S(2)}) async-start(), calls=%async_computation.16 | async-start | bytes 3145728 | tf_op jit(solution)/shard_map/psum | solution.py:135
  73.6 270.9 %all-gather.16.cloned.1.call-start = ((), (), s32[]{:S(2)}) async-start(), calls=%async_computation.17 | async-start | bytes 28311552 | tf_op jit(solution)/shard_map/all_gather | solution.py:68
  74.2 765.2 %all-reduce.23.cloned.1.call-start = ((), (), s32[]{:S(2)}) async-start(), calls=%async_computation.18 | async-start | bytes 3145728 | tf_op jit(solution)/shard_map/psum | solution.py:231
  795.7 130.0 %reduce-scatter.21.cloned.1.call-start = ((), (), s32[]{:S(2)}) async-start(), calls=%async_computation.20 | async-start | bytes 655360 | tf_op jit(solution)/shard_map/reduce_scatter | solution.py:298
  858.6 69.5 %reduce-scatter.19.cloned.1.call-start = ((), (), s32[]{:S(2)}) async-start(), calls=%async_computation.19 | async-start | bytes 655360 | tf_op jit(solution)/shard_map/reduce_scatter | solution.py:292
  866.8 71.7 %reduce-scatter.35.cloned.1.call-start = ((), (), s32[]{:S(2)}) async-start(), calls=%async_computation.28 | async-start | bytes 3538944 | tf_op jit(solution)/shard_map/reduce_scatter | solution.py:343
  868.8 106.8 %reduce-scatter.23.cloned.1.call-start = ((), (), s32[]{:S(2)}) async-start(), calls=%async_computation.21 | async-start | bytes 3538944 | tf_op jit(solution)/shard_map/reduce_scatter | solution.py:340
  875.6 516.1 %reduce-scatter.39.cloned.1.call-start = ((), (), s32[]{:S(2)}) async-start(), calls=%async_computation.31 | async-start | bytes 56623104 | tf_op jit(solution)/shard_map/reduce_scatter | solution.py:241
  923.6 481.0 %reduce-scatter.37.cloned.1.call-start = ((), (), s32[]{:S(2)}) async-start(), calls=%async_computation.30 | async-start | bytes 147456 | tf_op jit(solution)/shard_map/reduce_scatter | solution.py:344
  925.6 499.1 %reduce-scatter.31.cloned.1.call-start = ((), (), s32[]{:S(2)}) async-start(), calls=%async_computation.26 | async-start | bytes 1179648 | tf_op jit(solution)/shard_map/reduce_scatter | solution.py:342
  928.0 517.1 %reduce-scatter.27.cloned.1.call-start = ((), (), s32[]{:S(2)}) async-start(), calls=%async_computation.24 | async-start | bytes 1179648 | tf_op jit(solution)/shard_map/reduce_scatter | solution.py:341
  931.4 545.6 %reduce-scatter.43.cloned.1.call-start = ((), (), s32[]{:S(2)}) async-start(), calls=%async_computation.34 | async-start | bytes 1474560
  941.2 565.9 %reduce-scatter.25.cloned.1.call-start = ((), (), s32[]{:S(2)}) async-start(), calls=%async_computation.22 | async-start | bytes 1474560 | tf_op jit(solution)/shard_map/reduce_scatter | solution.py:359
  975.7 846.2 %reduce-scatter.41.cloned.1.call-start = ((), (), s32[]{:S(2)}) async-start(), calls=%async_computation.32 | async-start | bytes 23592960 | tf_op jit(solution)/shard_map/reduce_scatter | solution.py:356
  1391.8 454.0 %reduce-scatter.45.cloned.1.call-start = ((), (), s32[]{:S(2)}) async-start(), calls=%async_computation.35 | async-start | bytes 491520
  1406.3 509.8 %all-reduce.25.cloned.1.call-start = ((), (), s32[]{:S(2)}) async-start(), calls=%async_computation.36 | async-start | bytes 6291456 | tf_op jit(solution)/shard_map/psum | solution.py:193
  1410.9 567.5 %reduce-scatter.33.cloned.1.call-start = ((), (), s32[]{:S(2)}) async-start(), calls=%async_computation.27 | async-start | bytes 491520 | tf_op jit(solution)/shard_map/reduce_scatter | solution.py:361
  1424.7 571.7 %reduce-scatter.29.cloned.1.call-start = ((), (), s32[]{:S(2)}) async-start(), calls=%async_computation.25 | async-start | bytes 491520 | tf_op jit(solution)/shard_map/reduce_scatter | solution.py:360
  1445.1 565.8 %all-gather.20.cloned.1.call-start = ((), (), s32[]{:S(2)}) async-start(), calls=%async_computation.29 | async-start | bytes 1474560 | tf_op jit(solution)/shard_map/all_gather | solution.py:381
  1477.0 554.4 %all-gather.18.cloned.1.call-start = ((), (), s32[]{:S(2)}) async-start(), calls=%async_computation.23 | async-start | bytes 1474560 | tf_op jit(solution)/shard_map/all_gather | solution.py:378
  1507.1 847.6 %all-gather.22.cloned.1.call-start = ((), (), s32[]{:S(2)}) async-start(), calls=%async_computation.33 | async-start | bytes 23592960 | tf_op jit(solution)/shard_map/all_gather | solution.py:375
  2031.4 342.0 %copy-start.25 = (f32[768,384]{1,0:T(8,128)S(1)}, f32[768,384]{1,0:T(8,128)}, u32[]{:S(2)}) copy-start(f32[768,384]{1,0:T(8,128)} %all-gather.18.cloned.1.call-done) | copy-start | bytes 3538948
  (117 other events, 998.5 us)
Sparse Core Ops, SparseCore 0:
  9.6 25.4 all-gather.11
  36.6 23.5 all-gather.13
  73.7 44.8 all-reduce.20
  120.0 224.4 all-gather.15
  795.8 43.6 all-reduce.22
  858.7 21.6 reduce-scatter.20
  883.3 19.9 reduce-scatter.18
  905.5 32.9 reduce-scatter.34
  940.9 34.6 reduce-scatter.22
  977.8 413.8 reduce-scatter.38
  1394.5 9.9 reduce-scatter.36
  1407.2 17.4 reduce-scatter.30
  1427.6 17.4 reduce-scatter.26
  1447.8 29.1 reduce-scatter.42
  1479.2 27.8 reduce-scatter.24
  1509.3 312.4 reduce-scatter.40
  1824.1 21.6 reduce-scatter.44
  1849.2 66.8 all-reduce.24
  1918.4 20.9 reduce-scatter.32
  1941.6 18.7 reduce-scatter.28
  1962.0 37.5 all-gather.19
  2001.1 30.2 all-gather.17
  2033.0 321.6 all-gather.21
where the time goes:
time: 2400 us; the launch traced here: 2380 us
  waiting for transfers between devices  1530 us (64%)
  other arithmetic  292 us (12%)
  matrix products  195 us (8%)
  local copies, waits for them, and re-layouts  175 us (7%)
  blocking collectives  167 us (7%)
    reduce_scatter x1, waiting for transfers between devices, per_device(): lax.psum_scatter(jnp.concatenate([gate_terms, down_terms[:, None]], 1), '...  416 us
    all_gather x1, waiting for transfers between devices, per_device(): lax.all_gather(expert_piece, 'context', axis=2, tiled=True)  323 us
    reduce_scatter x1, waiting for transfers between devices, per_device(): lax.psum_scatter(expert_grad_part, 'context', scatter_dimension=2, tiled=...  315 us
    all_gather x1, waiting for transfers between devices, per_device(): w_experts = lax.all_gather(expert_weights, 'fsdp', axis=0, tiled=True)  202 us
    dynamic_update_slice x48, other arithmetic, per_device(): lax.scan(expert_backward, jnp.zeros((rows_count + 1, model_width), jnp.fl...  82 us
    scatter-add x16, other arithmetic, expert_forward(): running = running.at[slot_tokens].add(slot_gates[:, None] * produced)  76.9 us
    psum x1, waiting for transfers between devices, per_device(): lax.psum((ffn_part[:rows_count].reshape(tree_count, local_len, model_widt...  55.5 us
    unnamed x25, waiting for transfers between devices  54.3 us
  transfers between devices with their start and end apart: 23, of which 16 were waited for; matrix products, arithmetic and copies ran while one was open for 7% of the time, Pallas kernels for 0%

commit v1 on v0

v1 whole, which is shorter than its diff:
```python
import jax
import jax.numpy as jnp
from jax import lax
from jax.sharding import PartitionSpec as P

HEAD_DIM = 64
SEG = 128
EPS = 1e-06
BF = jnp.bfloat16
F32 = jnp.float32


def ancestry(parents):
    blocks = parents.shape[-1]
    diagonal = jnp.eye(blocks, dtype=jnp.int32)
    upward = (parents[..., :, None] == jnp.arange(blocks, dtype=jnp.int32)).astype(jnp.int32)
    closure = jnp.minimum(diagonal + upward, 1)
    for squaring in range(blocks.bit_length()):
        closure = jnp.minimum(jnp.matmul(closure, closure), 1)
    return closure


def dot(spec, a, b):
    return jnp.einsum(spec, a, b, preferred_element_type=F32)


def swap_halves(u):
    half = u.shape[-1] // 2
    return jnp.concatenate([-u[..., half:], u[..., :half]], -1)


def norm_scale(z):
    return lax.rsqrt(jnp.mean(z * z, -1, keepdims=True) + EPS)


def norm_back(z, scale, gain, grad):
    u = grad * gain
    out = scale * u - z * (scale**3) * jnp.mean(u * z, -1, keepdims=True)
    return out, jnp.sum(grad * z * scale, 0)


def per_device(
    residual_in,
    token_mask,
    parent_blocks,
    expert_routes,
    attn_gain,
    query_weight,
    key_weight,
    value_weight,
    output_weight,
    ffn_gain,
    router_weight,
    expert_weights,
    out_cotangent,
):
    _, rows, width = residual_in.shape
    tree_len = token_mask.shape[1]
    blocks = parent_blocks.shape[1]
    experts_here = expert_weights.shape[0]
    ctx = lax.axis_index("context")
    fs = lax.axis_index("fsdp")
    n_fs = lax.axis_size("fsdp")
    n_ctx = lax.axis_size("context")
    experts = experts_here * n_fs

    stream = residual_in[0].astype(F32)
    cot = out_cotangent[0]
    cot_all = lax.all_gather(cot.astype(BF), ("fsdp", "context"), axis=0, tiled=True)
    gain_one = lax.all_gather(attn_gain, "fsdp", axis=0, tiled=True).astype(F32)
    gain_two = lax.all_gather(ffn_gain, "fsdp", axis=0, tiled=True).astype(F32)
    w_qkv = jnp.concatenate([query_weight, key_weight, value_weight], 1)
    w_qkv = lax.all_gather(w_qkv, "fsdp", axis=0, tiled=True)
    w_out = lax.all_gather(output_weight, "fsdp", axis=1, tiled=True)
    w_router = lax.all_gather(router_weight, "fsdp", axis=0, tiled=True)

    heads = query_weight.shape[1] // HEAD_DIM
    kv = key_weight.shape[1] // HEAD_DIM
    group = heads // kv
    q_cols, kv_cols = heads * HEAD_DIM, kv * HEAD_DIM

    positions = ctx * rows + jnp.arange(rows, dtype=jnp.int32)
    pick = (positions[:, None] // SEG == jnp.arange(blocks, dtype=jnp.int32)[None, :]).astype(jnp.int32)
    closure = ancestry(parent_blocks[0])
    row_reach = jnp.matmul(pick, closure)
    depth = jnp.matmul(pick, jnp.sum(closure, -1) - 1)
    rope_pos = (depth * SEG + positions % SEG).astype(F32)
    half_freq = 10000.0 ** (-(jnp.arange(HEAD_DIM // 2, dtype=F32) * 2.0) / HEAD_DIM)
    angles = rope_pos[:, None, None] * jnp.concatenate([half_freq, half_freq])
    cos, sin = jnp.cos(angles), jnp.sin(angles)
    key_pos = jnp.arange(tree_len, dtype=jnp.int32)
    allowed = (
        (jnp.repeat(row_reach, SEG, axis=1) > 0)
        & (key_pos[None, :] <= positions[:, None])
        & (token_mask[0][None, :] > 0)
    )

    scale_one = norm_scale(stream)
    normed_one = (stream * scale_one * gain_one).astype(BF)
    qkv = dot("ld,dc->lc", normed_one, w_qkv)

    def rot(u):
        u = u.reshape(rows, -1, HEAD_DIM)
        return (u * cos + swap_halves(u) * sin).astype(BF).reshape(rows, -1)

    def unrot(u):
        u = u.reshape(rows, -1, HEAD_DIM)
        return (u * cos - swap_halves(u) * sin).astype(BF).reshape(rows, -1)

    q = rot(qkv[:, :q_cols]).reshape(rows, kv, group, HEAD_DIM)
    k_own = rot(qkv[:, q_cols : q_cols + kv_cols])
    v_own = qkv[:, q_cols + kv_cols :].astype(BF)
    kv_all = lax.all_gather(jnp.concatenate([k_own, v_own], 1), "context", axis=0, tiled=True)
    k_all = kv_all[:, :kv_cols].reshape(tree_len, kv, HEAD_DIM)
    v_all = kv_all[:, kv_cols:].reshape(tree_len, kv, HEAD_DIM)

    scores = dot("lkgh,mkh->kglm", q, k_all) * 0.125
    masked = jnp.where(allowed, scores, -jnp.inf)
    peak = jnp.max(masked, -1, keepdims=True)
    log_total = peak + jnp.log(jnp.sum(jnp.exp(masked - peak), -1, keepdims=True))
    probs = jnp.exp(masked - log_total)
    probs_low = probs.astype(BF)
    attended = dot("kglm,mkh->lkgh", probs_low, v_all).astype(BF).reshape(rows, q_cols)
    attn_out = lax.psum(dot("lc,cd->ld", attended, w_out).astype(BF), "tensor").astype(F32)
    middle = stream + attn_out
    scale_two = norm_scale(middle)
    normed_two = (middle * scale_two * gain_two).astype(BF)

    logits = dot("ld,de->le", normed_two, w_router)
    router_probs = jax.nn.softmax(logits, -1)
    routes = expert_routes[0]
    used = jnp.any(routes[:, :, None] == jnp.arange(experts, dtype=jnp.int32), 1)
    gates = jnp.where(used, router_probs, 0.0)

    normed_all = lax.all_gather(normed_two, ("fsdp", "context"), axis=0, tiled=True)
    gates_all = lax.all_gather(gates, ("fsdp", "context"), axis=0, tiled=True)
    gates_here = lax.dynamic_slice_in_dim(gates_all, fs * experts_here, experts_here, 1)
    g3 = gates_here[:, :, None]
    gate_val = dot("td,edf->tef", normed_all, expert_weights[:, 0])
    up_val = dot("td,edf->tef", normed_all, expert_weights[:, 1])
    back = dot("td,edf->tef", cot_all, expert_weights[:, 2])
    sig = 1.0 / (1.0 + jnp.exp(-gate_val))
    act = gate_val * sig
    hid = act * up_val
    gated_hid = (g3 * hid).astype(BF)
    gate_grad_part = jnp.sum(hid * back, -1)
    d_hid = g3 * back
    d_gate_val = (d_hid * up_val * (sig * (1.0 + gate_val * (1.0 - sig)))).astype(BF)
    d_up_val = (d_hid * act).astype(BF)

    def own(z):
        z = z.reshape((n_fs, n_ctx, rows) + z.shape[1:])
        return lax.dynamic_index_in_dim(z, ctx, 1, keepdims=False)

    ffn_part = dot("stef,edf->std", own(gated_hid), expert_weights[:, 2])
    dn_part = dot("stef,edf->std", own(d_gate_val), expert_weights[:, 0]) + dot(
        "stef,edf->std", own(d_up_val), expert_weights[:, 1]
    )
    gate_part = lax.dynamic_update_slice_in_dim(
        jnp.zeros((n_fs, rows, experts), F32), own(gate_grad_part), fs * experts_here, 2
    )

    def home(z):
        z = lax.psum_scatter(z.astype(BF), "fsdp", scatter_dimension=0, tiled=True)
        return lax.psum(z, "tensor").astype(F32)[0]

    dn = home(dn_part)
    gate_grad = lax.psum(lax.psum_scatter(gate_part, "fsdp", scatter_dimension=0, tiled=True), "tensor")[0]
    ffn_out = home(ffn_part)
    block_out = middle + ffn_out

    expert_grad = jnp.stack(
        [
            dot("td,tef->edf", normed_all, d_gate_val),
            dot("td,tef->edf", normed_all, d_up_val),
            dot("td,tef->edf", cot_all, gated_hid),
        ],
        1,
    )

    own_mask = lax.dynamic_slice_in_dim(token_mask[0], ctx * rows, rows, 0).astype(F32)
    sums = [jnp.sum(jnp.sum(z * z, -1) * own_mask) for z in (stream, attn_out, middle, ffn_out)]
    sums = lax.psum(jnp.stack(sums + [jnp.sum(own_mask)]), ("fsdp", "context"))
    rms_stats = jnp.sqrt(sums[:4] / (sums[4] * width))

    prob_grad = jnp.where(used, gate_grad, 0.0)
    logit_grad = (router_probs * (prob_grad - jnp.sum(router_probs * prob_grad, -1, keepdims=True))).astype(BF)
    dn = dn + dot("le,de->ld", logit_grad, w_router)
    router_full = dot("ld,le->de", normed_two, logit_grad)
    mid_grad, ffn_gain_full = norm_back(middle, scale_two, gain_two, dn)
    middle_grad = cot + mid_grad
    d_attn = middle_grad.astype(BF)
    out_full = dot("lc,ld->cd", attended, d_attn)
    d_att = dot("ld,cd->lc", d_attn, w_out).astype(BF).reshape(rows, kv, group, HEAD_DIM)
    d_probs = dot("lkgh,mkh->kglm", d_att, v_all)
    delta = jnp.sum(probs * d_probs, -1, keepdims=True)
    d_scores = (probs * (d_probs - delta)).astype(BF)
    dq = dot("kglm,mkh->lkgh", d_scores, k_all) * 0.125
    dk = dot("kglm,lkgh->mkh", d_scores, q) * 0.125
    dv = dot("kglm,lkgh->mkh", probs_low, d_att)
    dkv = jnp.concatenate([dk.reshape(tree_len, kv_cols), dv.reshape(tree_len, kv_cols)], 1)
    dkv = lax.psum_scatter(dkv.astype(BF), "context", scatter_dimension=0, tiled=True).astype(F32)
    d_qkv = jnp.concatenate(
        [unrot(dq.reshape(rows, q_cols)), unrot(dkv[:, :kv_cols]), dkv[:, kv_cols:].astype(BF)], 1
    )
    qkv_full = dot("ld,lc->dc", normed_one, d_qkv)
    dn_one = lax.psum(dot("lc,dc->ld", d_qkv, w_qkv).astype(BF), "tensor").astype(F32)
    str_grad, attn_gain_full = norm_back(stream, scale_one, gain_one, dn_one)
    input_grad = middle_grad + str_grad

    qkv_part = lax.psum(lax.psum_scatter(qkv_full.astype(BF), "fsdp", scatter_dimension=0, tiled=True), "context").astype(F32)
    out_part = lax.psum(lax.psum_scatter(out_full.astype(BF), "fsdp", scatter_dimension=1, tiled=True), "context").astype(F32)
    small = jnp.concatenate([router_full, attn_gain_full[:, None], ffn_gain_full[:, None]], 1)
    small = lax.psum(lax.psum_scatter(small, "fsdp", scatter_dimension=0, tiled=True), "context")
    return (
        block_out.astype(BF)[None],
        input_grad[None],
        small[:, experts],
        qkv_part[:, :q_cols],
        qkv_part[:, q_cols : q_cols + kv_cols],
        qkv_part[:, q_cols + kv_cols :],
        out_part,
        small[:, experts + 1],
        small[:, :experts],
        expert_grad,
        rms_stats,
    )


def solution(mesh):
    return jax.shard_map(
        per_device,
        mesh=mesh,
        in_specs=(
            P("fsdp", "context", None),
            P("fsdp", None),
            P("fsdp", None),
            P("fsdp", "context", None),
            P("fsdp"),
            P("fsdp", "tensor"),
            P("fsdp", "tensor"),
            P("fsdp", "tensor"),
            P("tensor", "fsdp"),
            P("fsdp"),
            P("fsdp", None),
            P("fsdp", None, None, "tensor"),
            P("fsdp", "context", None),
        ),
        out_specs=(
            P("fsdp", "context", None),
            P("fsdp", "context", None),
            P("fsdp"),
            P("fsdp", "tensor"),
            P("fsdp", "tensor"),
            P("fsdp", "tensor"),
            P("tensor", "fsdp"),
            P("fsdp"),
            P("fsdp", None),
            P("fsdp", None, None, "tensor"),
            P(),
        ),
        check_vma=False,
    )
```

time: 2400 us -> 665 us (0.28)
  waiting for transfers between devices: 1530 us -> 334 us
  other arithmetic: 292 us -> 39.6 us
  local copies, waits for them, and re-layouts: 175 us -> 34.8 us
  matrix products: 195 us -> 117 us
  blocking collectives: 167 us -> 114 us
    reduce_scatter x12 -> x7, waiting for transfers between devices: 846 us -> 117 us  [the longest x2 45.8 us: home(): z = lax.psum_scatter(z.astype(BF), 'fsdp', scatter_dimension=0, tiled=True)]
    all_gather x6 -> x4, waiting for transfers between devices: 543 us -> 139 us  [the longest x1 88.7 us: per_device(): lax.all_gather(normed_two, ('fsdp', 'context'), axis=0, tiled=True)]
    scatter-add x32 -> x0, other arithmetic: 130 us -> none  [the longest x16 76.9 us: expert_forward(): running = running.at[slot_tokens].add(slot_gates[:, None] * produced)]
    dynamic_update_slice x48 -> x0, other arithmetic: 82 us -> none  [per_device(): lax.scan(expert_backward, jnp.zeros((rows_count + 1, model_width), jnp.fl...]
    gather x34 -> x0, local copies, waits for them, and re-layouts: 81.9 us -> none  [the longest x16 30.2 us: expert_backward(): padded_cot[slot_tokens]]
    dot_general x89 -> x26, matrix products: 195 us -> 115 us  [the longest x24 115 us: dot(): return jnp.einsum(spec, a, b, preferred_element_type=F32)]
    unnamed x25 -> x15, waiting for transfers between devices: 54.3 us -> 0.93 us
    all_gather x10 -> x5, blocking collectives: 104 us -> 61.3 us  [the longest x1 31.9 us: per_device(): gates_all = lax.all_gather(gates, ('fsdp', 'context'), axis=0, tiled=True)]
  transfers between devices with their start and end apart: 23 -> 15, of which waited for: 16 -> 14; matrix products, arithmetic and copies ran while one was open for 7% -> 19% of each run, Pallas kernels for 0% -> 0%
where the time goes in v1:
time: 665 us; the launch traced here: 657 us
  waiting for transfers between devices  334 us (50%)
  matrix products  117 us (18%)
  blocking collectives  114 us (17%)
  other arithmetic  39.6 us (6%)
  local copies, waits for them, and re-layouts  34.8 us (5%)
  between operations  16.9 us (3%)
    dot_general x24, matrix products, dot(): return jnp.einsum(spec, a, b, preferred_element_type=F32)  115 us
    all_gather x1, waiting for transfers between devices, per_device(): lax.all_gather(normed_two, ('fsdp', 'context'), axis=0, tiled=True)  88.7 us
    reduce_scatter x2, waiting for transfers between devices, home(): z = lax.psum_scatter(z.astype(BF), 'fsdp', scatter_dimension=0, tiled=True)  45.8 us
    psum x2, waiting for transfers between devices, home(): return lax.psum(z, 'tensor').astype(F32)[0]  42.7 us
    reduce_scatter x1, waiting for transfers between devices, per_device(): lax.psum_scatter(qkv_full.astype(BF), 'fsdp', scatter_dimension=0, tiled=...  32.8 us
    all_gather x1, blocking collectives, per_device(): gates_all = lax.all_gather(gates, ('fsdp', 'context'), axis=0, tiled=True)  31.9 us
    psum x1, waiting for transfers between devices, per_device(): lax.psum(dot('lc,cd->ld', attended, w_out).astype(BF), 'tensor').astype(F32)  28.9 us
    all_gather x1, waiting for transfers between devices, per_device(): w_qkv = lax.all_gather(w_qkv, 'fsdp', axis=0, tiled=True)  25.2 us
  transfers between devices with their start and end apart: 15, of which 14 were waited for; matrix products, arithmetic and copies ran while one was open for 19% of the time, Pallas kernels for 0%

profile of v1, /device:TPU:0, one launch (start us, length us, event | category | flops | bytes accessed | tf_op | source)
XLA Modules:
  0.0 657.2 jit_solution(3967643498677726864)
XLA Ops:
  20.4 25.2 %all-gather.7.cloned.1.call-done = bf16[1536,640]{1,0:T(8,128)(2,1)} async-done(((bf16[768,640]{1,0:T(8,128)(2,1)}), bf16[1536,640]{1,0:T(8,128)(2,1)}) %all-gather.7.cloned.1.call-update) | async-done | bytes 1966096 | tf_op jit(solution)/shard_map/all_gather | solution.py:73
  48.3 15.3 %all_gather.29 = bf16[1024,256]{1,0:T(8,128)(2,1)S(1)} all-gather(bf16[256,256]{1,0:T(8,128)(2,1)S(1)} %pad_maximum_fusion.7), channel_id=1, replica_groups=mesh['fsdp'=2,'context'=4,'tensor'=4] {'context'}, dimensions={0}, use_global_device_ids=true | all-gather | bytes 655360 | tf_op jit(solution)/shard_map/all_gather | solution.py:113
  79.5 28.9 %all-reduce.7.cloned.1.call-done = bf16[256,1536]{1,0:T(8,128)(2,1)} async-done(((bf16[256,1536]{1,0:T(8,128)(2,1)}), bf16[256,1536]{1,0:T(8,128)(2,1)}) %all-reduce.7.cloned.1.call-update) | async-done | bytes 786448 | tf_op jit(solution)/shard_map/psum | solution.py:124
  118.3 31.9 %all_gather.33 = f32[2048,16]{0,1:T(8,128)S(1)} all-gather(f32[256,16]{0,1:T(8,128)S(1)} %broadcast_select_fusion.1), channel_id=1, replica_groups=mesh['fsdp'=2,'context'=4,'tensor'=4] {'fsdp','context'}, dimensions={0}, use_global_device_ids=true | all-gather | bytes 147456 | tf_op jit(solution)/shard_map/all_gather | solution.py:136
  150.2 25.0 %all-gather.13.cloned.1.call-done = bf16[2048,1536]{1,0:T(8,128)(2,1)} async-done(((bf16[256,1536]{1,0:T(8,128)(2,1)}), bf16[2048,1536]{1,0:T(8,128)(2,1)}) %all-gather.13.cloned.1.call-update) | async-done | bytes 6291472 | tf_op jit(solution)/shard_map/all_gather | solution.py:69
  175.2 12.1 %fusion.6 = f32[2048,8,128]{2,0,1:T(8,128)} fusion(bf16[2048,1536]{1,0:T(8,128)(2,1)} %all-gather.13.cloned.1.call-done, bf16[8,3,1536,128]{3,2,1,0:T(8,128)(2,1)} %param.24), kind=kOutput, calls=%fused_computation.14 | convolution fusion | flops 6442450944 | bytes 17825792 | tf_op jit(solution)/shard_map/td,edf->tef/dot_general | solution.py:24
  187.4 88.7 %all-gather.11.cloned.1.call-done = bf16[2048,1536]{1,0:T(8,128)(2,1)} async-done(((bf16[256,1536]{1,0:T(8,128)(2,1)}), bf16[2048,1536]{1,0:T(8,128)(2,1)}) %all-gather.11.cloned.1.call-update) | async-done | bytes 6291472 | tf_op jit(solution)/shard_map/all_gather | solution.py:135
  276.1 12.3 %fusion.12 = f32[2048,8,128]{2,0,1:T(8,128)} fusion(bf16[2048,1536]{1,0:T(8,128)(2,1)} %all-gather.11.cloned.1.call-done, bf16[8,3,1536,128]{3,2,1,0:T(8,128)(2,1)} %param.24), kind=kOutput, calls=%fused_computation.20 | convolution fusion | flops 6442450944 | bytes 17825792 | tf_op jit(solution)/shard_map/td,edf->tef/dot_general | solution.py:24
  288.4 16.2 %multiply_convert_fusion.1 = (bf16[2048,8,128]{2,0,1:T(8,128)(2,1)}, f32[2048,8]{0,1:T(8,128)S(1)}, bf16[2048,8,128]{2,0,1:T(8,128)(2,1)S(1)}, bf16[2048,8,128]{2,0,1:T(8,128)(2,1)}) fusion(f32[2048,8,128]{2,0,1:T(8,128)} %fusion.12, f32[2048,8,128]{2,0,1:T(8,128)} %fusion.6, f32[2048,8]{0,1:T(8,128)S(1)} %constant_dynamic-slice_fusion.4, ...), kind=kOutput, calls=%fused_computation.3 | convolution fusion | flops 6482280448 | bytes 38928384 | tf_op jit(solution)/shard_map/td,edf->tef/dot_general | solution.py:24
  311.6 23.6 %reduce-scatter.10.cloned.1.call-done = bf16[1,256,1536]{2,1,0:T(8,128)(2,1)} async-done(((bf16[2,256,1536]{2,1,0:T(8,128)(2,1)}), bf16[1,256,1536]{2,1,0:T(8,128)(2,1)}) %reduce-scatter.10.cloned.1.call-update) | async-done | bytes 786448 | tf_op jit(solution)/shard_map/reduce_scatter | solution.py:164
  335.4 12.4 %reduce-scatter.12.cloned.1.call-done = f32[1,256,16]{1,2,0:T(8,128)} async-done(((f32[2,256,16]{1,2,0:T(8,128)}), f32[1,256,16]{1,2,0:T(8,128)}) %reduce-scatter.12.cloned.1.call-update) | async-done | bytes 16400 | tf_op jit(solution)/shard_map/reduce_scatter | solution.py:168
  347.8 11.7 %psum.66 = f32[256,16]{0,1:T(8,128)S(1)} all-reduce(f32[256,16]{0,1:T(8,128)} %bitcast.270), channel_id=1, replica_groups=mesh['fsdp'=2,'context'=4,'tensor'=4] {'tensor'}, use_global_device_ids=true, to_apply=%region_15.16 | all-reduce | flops 4096 | bytes 32768 | tf_op jit(solution)/shard_map/psum | solution.py:168
  359.5 25.4 %all-reduce.9.cloned.1.call-done = bf16[256,1536]{1,0:T(8,128)(2,1)} async-done(((bf16[256,1536]{1,0:T(8,128)(2,1)}), bf16[256,1536]{1,0:T(8,128)(2,1)}) %all-reduce.9.cloned.1.call-update) | async-done | bytes 786448 | tf_op jit(solution)/shard_map/psum | solution.py:165
  410.4 15.5 %reduce-scatter.14.cloned.1.call-done = bf16[256,256]{0,1:T(8,128)(2,1)} async-done(((bf16[1024,256]{0,1:T(8,128)(2,1)}), bf16[256,256]{0,1:T(8,128)(2,1)}) %reduce-scatter.14.cloned.1.call-update) | async-done | bytes 131088 | tf_op jit(solution)/shard_map/reduce_scatter | solution.py:202
  431.1 22.1 %reduce-scatter.8.cloned.1.call-done = bf16[1,256,1536]{2,1,0:T(8,128)(2,1)} async-done(((bf16[2,256,1536]{2,1,0:T(8,128)(2,1)}), bf16[1,256,1536]{2,1,0:T(8,128)(2,1)}) %reduce-scatter.8.cloned.1.call-update) | async-done | bytes 786448 | tf_op jit(solution)/shard_map/reduce_scatter | solution.py:164
  458.9 12.2 %fusion.17 = f32[8,1,1536,128]{2,3,0,1:T(8,128)} fusion(bf16[2048,8,128]{2,0,1:T(8,128)(2,1)} %get-tuple-element.72, bf16[2048,1536]{1,0:T(8,128)(2,1)} %all-gather.11.cloned.1.call-done), kind=kOutput, calls=%fused_computation.28 | convolution fusion | flops 6442450944 | bytes 16777216 | tf_op jit(solution)/shard_map/td,tef->edf/dot_general | solution.py:24
  471.1 10.7 %fusion.20 = f32[8,1,1536,128]{2,3,0,1:T(8,128)} fusion(bf16[2048,8,128]{2,0,1:T(8,128)(2,1)S(1)} %copy-done.34, bf16[2048,1536]{1,0:T(8,128)(2,1)} %all-gather.11.cloned.1.call-done), kind=kOutput, calls=%fused_computation.29 | convolution fusion | flops 6442450944 | bytes 16777216 | tf_op jit(solution)/shard_map/td,tef->edf/dot_general | solution.py:24
  482.0 17.3 %all-reduce.11.cloned.1.call-done = (bf16[256,1536]{1,0:T(8,128)(2,1)}, bf16[256,1536]{1,0:T(8,128)(2,1)}) async-done(((bf16[256,1536]{1,0:T(8,128)(2,1)}, bf16[256,1536]{1,0:T(8,128)(2,1)}), (bf16[256,1536]{1,0:T(8,128)(2,1)}, bf16[256,1536]{1,0:T(8,128)(2,1)})) %all-reduce.11.cloned.1.call-update) | async-done | bytes 1572880 | tf_op jit(solution)/shard_map/psum | solution.py:165
  501.8 11.8 %fusion.23 = f32[8,1,1536,128]{2,3,0,1:T(8,128)} fusion(bf16[2048,8,128]{2,0,1:T(8,128)(2,1)} %get-tuple-element.75, bf16[2048,1536]{1,0:T(8,128)(2,1)} %all-gather.13.cloned.1.call-done), kind=kOutput, calls=%fused_computation.30 | convolution fusion | flops 6442450944 | bytes 16777216 | tf_op jit(solution)/shard_map/td,tef->edf/dot_general | solution.py:24
  523.8 32.8 %reduce-scatter.18.cloned.1.call-done = bf16[768,640]{1,0:T(8,128)(2,1)} async-done(((bf16[1536,640]{1,0:T(8,128)(2,1)}), bf16[768,640]{1,0:T(8,128)(2,1)}) %reduce-scatter.18.cloned.1.call-update) | async-done | bytes 983056 | tf_op jit(solution)/shard_map/reduce_scatter | solution.py:211
  556.6 13.5 %pad_maximum_fusion = f32[8,3,1536,128]{2,3,0,1:T(8,128)} fusion(f32[8,1,1536,128]{2,3,0,1:T(8,128)} %fusion.23, f32[8,1,1536,128]{2,3,0,1:T(8,128)} %fusion.20, f32[8,1,1536,128]{2,3,0,1:T(8,128)} %fusion.17), kind=kLoop, calls=%fused_computation | loop fusion | flops 9437184 | bytes 37748736 | tf_op jit(solution)/shard_map/stack | solution.py:172
  576.2 18.7 %copy.121 = f32[8,3,1536,128]{3,2,1,0:T(8,128)} copy(f32[8,3,1536,128]{2,3,0,1:T(8,128)} %pad_maximum_fusion) | data formatting | bytes 37748736
  594.9 21.0 %psum.71 = f32[5]{0:T(128)S(1)} all-reduce(f32[5]{0:T(128)S(1)} %stack.39), channel_id=1, replica_groups=mesh['fsdp'=2,'context'=4,'tensor'=4] {'fsdp','context'}, use_global_device_ids=true, to_apply=%region_37.38 | all-reduce | flops 5 | bytes 40 | tf_op jit(solution)/shard_map/psum | solution.py:183
  617.7 19.9 %psum.68 = f32[768,18]{0,1:T(8,128)S(1)} all-reduce(f32[768,18]{0,1:T(8,128)} %reduce-scatter.16.cloned.1.call-done), channel_id=1, replica_groups=mesh['fsdp'=2,'context'=4,'tensor'=4] {'context'}, use_global_device_ids=true, to_apply=%region_25.26 | all-reduce | flops 13824 | bytes 110592 | tf_op jit(solution)/shard_map/psum | solution.py:214
  (216 shorter events, 116.0 us)
Async XLA Ops:
  8.0 37.5 %all-gather.7.cloned.1.call-start = ((), (), s32[]{:S(2)}) async-start(), calls=%async_computation.7 | async-start | bytes 2949120 | tf_op jit(solution)/shard_map/all_gather | solution.py:73
  10.5 59.3 %all-gather.9.cloned.1.call-start = ((), (), s32[]{:S(2)}) async-start(), calls=%async_computation.8 | async-start | bytes 1769472 | tf_op jit(solution)/shard_map/all_gather | solution.py:74
  11.2 97.2 %all-reduce.7.cloned.1.call-start = ((), (), s32[]{:S(2)}) async-start(), calls=%async_computation.9 | async-start | bytes 1572864 | tf_op jit(solution)/shard_map/psum | solution.py:124
  14.0 34.0 %copy-start.23 = (f32[256]{0:T(256)}, f32[256]{0:T(256)S(1)}, u32[]{:S(2)}) copy-start(f32[256]{0:T(256)S(1)} %get-tuple-element.96) | copy-start | bytes 3076
  69.7 42.5 %copy-start.12 = (bf16[2,64,3,256]{3,1,2,0:T(8,128)(2,1)}, bf16[2,64,3,256]{3,1,2,0:T(8,128)(2,1)S(1)}, u32[]{:S(2)}) copy-start(bf16[2,64,3,256]{3,1,2,0:T(8,128)(2,1)S(1)} %convolution_convert_fusion.5) | copy-start | bytes 589828
  72.6 39.7 %copy-start.18 = (bf16[768,16]{0,1:T(8,128)(2,1)S(1)}, bf16[768,16]{0,1:T(8,128)(2,1)}, u32[]{:S(2)}) copy-start(bf16[768,16]{0,1:T(8,128)(2,1)} %param.23) | copy-start | bytes 73732
  72.6 44.2 %copy-start.26 = (s32[1,256,8]{1,2,0:T(8,128)S(1)}, s32[1,256,8]{1,2,0:T(8,128)}, u32[]{:S(2)}) copy-start(s32[1,256,8]{1,2,0:T(8,128)} %param.16) | copy-start | bytes 24580
  72.6 102.7 %all-gather.13.cloned.1.call-start = ((), (), s32[]{:S(2)}) async-start(), calls=%async_computation.12 | async-start | bytes 7077888 | tf_op jit(solution)/shard_map/all_gather | solution.py:69
  75.0 201.0 %all-gather.11.cloned.1.call-start = ((), (), s32[]{:S(2)}) async-start(), calls=%async_computation.10 | async-start | bytes 7077888 | tf_op jit(solution)/shard_map/all_gather | solution.py:135
  112.2 223.1 %reduce-scatter.10.cloned.1.call-start = ((), (), s32[]{:S(2)}) async-start(), calls=%async_computation.13 | async-start | bytes 2359296 | tf_op jit(solution)/shard_map/reduce_scatter | solution.py:164
  276.1 28.5 %slice-start.2 = ((s8[9437184]{0:T(1024)(128)(4,1)}), s8[4194304]{0:T(1024)(128)(4,1)S(1)}, s32[]{:S(2)}) async-start(s8[9437184]{0:T(1024)(128)(4,1)} %bitcast.275), calls=%async_computation.24 | async-start | bytes 8388608
  276.1 28.5 %slice-start.3 = ((s8[9437184]{0:T(1024)(128)(4,1)}), s8[4194304]{0:T(1024)(128)(4,1)S(1)}, s32[]{:S(2)}) async-start(s8[9437184]{0:T(1024)(128)(4,1)} %bitcast.275), calls=%async_computation.25 | async-start | bytes 8388608
  306.6 78.3 %copy-start.8 = (bf16[256,1536]{1,0:T(8,128)(2,1)S(1)}, bf16[256,1536]{1,0:T(8,128)(2,1)}, u32[]{:S(2)}) copy-start(bf16[256,1536]{1,0:T(8,128)(2,1)} %all-reduce.7.cloned.1.call-done) | copy-start | bytes 2359300
  310.9 36.9 %reduce-scatter.12.cloned.1.call-start = ((), (), s32[]{:S(2)}) async-start(), calls=%async_computation.15 | async-start | bytes 49152 | tf_op jit(solution)/shard_map/reduce_scatter | solution.py:168
  311.6 73.3 %all-reduce.9.cloned.1.call-start = ((), (), s32[]{:S(2)}) async-start(), calls=%async_computation.14 | async-start | bytes 1572864 | tf_op jit(solution)/shard_map/psum | solution.py:165
  335.3 90.7 %reduce-scatter.14.cloned.1.call-start = ((), (), s32[]{:S(2)}) async-start(), calls=%async_computation.16 | async-start | bytes 655360 | tf_op jit(solution)/shard_map/reduce_scatter | solution.py:202
  404.1 49.1 %reduce-scatter.8.cloned.1.call-start = ((), (), s32[]{:S(2)}) async-start(), calls=%async_computation.11 | async-start | bytes 2359296 | tf_op jit(solution)/shard_map/reduce_scatter | solution.py:164
  409.5 89.8 %all-reduce.11.cloned.1.call-start = ((), (), s32[]{:S(2)}) async-start(), calls=%async_computation.20 | async-start | bytes 3145728 | tf_op jit(solution)/shard_map/psum | solution.py:165
  410.3 43.0 %copy-start.6 = (f32[256,1536]{1,0:T(8,128)S(1)}, f32[256,1536]{1,0:T(8,128)}, u32[]{:S(2)}) copy-start(f32[256,1536]{1,0:T(8,128)} %copy-done.5) | copy-start | bytes 4718596
  410.3 43.0 %copy-start.13 = (bf16[2,64,3,256]{3,1,2,0:T(8,128)(2,1)S(1)}, bf16[2,64,3,256]{3,1,2,0:T(8,128)(2,1)}, u32[]{:S(2)}) copy-start(bf16[2,64,3,256]{3,1,2,0:T(8,128)(2,1)} %copy-done.12) | copy-start | bytes 589828
  453.2 70.5 %reduce-scatter.20.cloned.1.call-start = ((), (), s32[]{:S(2)}) async-start(), calls=%async_computation.19 | async-start | bytes 1769472 | tf_op jit(solution)/shard_map/reduce_scatter | solution.py:212
  454.8 101.7 %reduce-scatter.18.cloned.1.call-start = ((), (), s32[]{:S(2)}) async-start(), calls=%async_computation.18 | async-start | bytes 2949120 | tf_op jit(solution)/shard_map/reduce_scatter | solution.py:211
  457.1 160.6 %reduce-scatter.16.cloned.1.call-start = ((), (), s32[]{:S(2)}) async-start(), calls=%async_computation.17 | async-start | bytes 221184 | tf_op jit(solution)/shard_map/reduce_scatter | solution.py:214
  501.6 143.0 %all-reduce.13.cloned.1.call-start = ((), (), s32[]{:S(2)}) async-start(), calls=%async_computation.21 | async-start | bytes 3145728 | tf_op jit(solution)/shard_map/psum | solution.py:211
  (31 other events, 255.9 us)
Sparse Core Ops, SparseCore 0:
  11.0 34.5 all-gather.6
  47.1 22.6 all-gather.8
  72.7 35.6 all-reduce.6
  311.0 24.2 reduce-scatter.9
  338.0 9.7 reduce-scatter.11
  350.1 34.6 all-reduce.8
  404.2 21.6 reduce-scatter.13
  428.9 24.3 reduce-scatter.7
  456.2 43.0 all-reduce.10
  502.0 21.7 reduce-scatter.19
  526.1 30.3 reduce-scatter.17
  559.2 10.4 reduce-scatter.15
  572.1 72.4 all-reduce.12
Sparse Core Ops, SparseCore 1:
  75.7 99.5 all-gather.12
  177.8 98.2 all-gather.10

commit v2 on v1

--- a/solution.py
+++ b/solution.py
@@ -1,6 +1,10 @@
+import functools
+
 import jax
 import jax.numpy as jnp
 from jax import lax
+from jax.experimental import pallas as pl
+from jax.experimental.pallas import tpu as pltpu
 from jax.sharding import PartitionSpec as P
 
 HEAD_DIM = 64
@@ -8,6 +12,364 @@
 EPS = 1e-06
 BF = jnp.bfloat16
 F32 = jnp.float32
+
+
+MESH = pl.DeviceIdType.MESH
+VM = pltpu.VMEM
+
+
+def tdot(a, b, dims):
+    return lax.dot_general(a, b, (dims, ((), ())), preferred_element_type=F32)
+
+
+NN = ((1,), (0,))
+NT = ((1,), (1,))
+TN = ((0,), (0,))
+
+
+def place():
+    f, c, t = lax.axis_index("fsdp"), lax.axis_index("context"), lax.axis_index("tensor")
+    core = lax.rem(t, 2)
+    peers = dict(
+        x=(1 - f, c, t), core=(f, c, t + 1 - 2 * core), y=(f, c, lax.rem(t + 2, 4))
+    )
+    return f, c, t, core, peers
+
+
+def greet(c, n_ctx, peers, f, t):
+    bar = pltpu.get_barrier_semaphore()
+    for p in peers.values():
+        pl.semaphore_signal(bar, inc=1, device_id=p, device_id_type=MESH)
+
+    @pl.when(c > 0)
+    def _():
+        pl.semaphore_signal(bar, inc=1, device_id=(f, c - 1, t), device_id_type=MESH)
+
+    @pl.when(c < n_ctx - 1)
+    def _():
+        pl.semaphore_signal(bar, inc=1, device_id=(f, c + 1, t), device_id_type=MESH)
+
+    near = jnp.where(c > 0, 1, 0) + jnp.where(c < n_ctx - 1, 1, 0)
+    pl.semaphore_wait(bar, len(peers) + near)
+
+
+def remote(src, dst, send, recv, device):
+    return pltpu.make_async_remote_copy(
+        src_ref=src, dst_ref=dst, send_sem=send, recv_sem=recv, device_id=device, device_id_type=MESH
+    )
+
+
+class Gather:
+    def __init__(self, buf, sems, n_ctx, where):
+        self.buf, self.n = buf, n_ctx
+        self.f, self.c, self.t, self.core, self.peers = where
+        self.half = buf.shape[2] // 2
+        self.zs, self.zr, self.xs, self.xr, self.ks, self.kr = sems
+
+    @staticmethod
+    def sems(n_ctx):
+        d = pltpu.SemaphoreType.DMA
+        return [d((2, n_ctx)), d((n_ctx,)), d((n_ctx,)), d((n_ctx,)), d((2, n_ctx)), d((2, n_ctx))]
+
+    def part(self, f, c, core):
+        return self.buf.at[f * self.n + c, :, pl.ds(pl.multiple_of(core * self.half, 128), self.half)]
+
+    def z(self, side, block):
+        r = self.part(self.f, block, self.core)
+        return remote(r, r, self.zs.at[(side + 1) // 2, block], self.zr.at[block], (self.f, self.c + side, self.t))
+
+    def x(self, block):
+        r = self.part(self.f, block, self.core)
+        return remote(r, r, self.xs.at[block], self.xr.at[block], self.peers["x"])
+
+    def k(self, f, block):
+        r = self.part(f, block, self.core)
+        return remote(r, r, self.ks.at[f, block], self.kr.at[f, block], self.peers["core"])
+
+    def there(self, c):
+        return (c >= 0) & (c < self.n)
+
+    def begin(self):
+        c = self.c
+        self.x(c).start()
+        for side in (-1, 1):
+            pl.when(self.there(c + side))(lambda side=side: self.z(side, c).start())
+
+    def relay(self, d):
+        for side in (-1, 1):
+            block = self.c + side * d
+
+            @pl.when(self.there(block))
+            def _(side=side, block=block):
+                self.z(-side, block).wait_recv()
+                pl.when(self.there(self.c - side))(lambda: self.z(-side, block).start())
+                self.x(block).start()
+                self.k(self.f, block).start()
+
+    def cross(self, block):
+        r = self.part(1 - self.f, block, self.core)
+        remote(r, r, self.xs.at[block], self.xr.at[block], self.peers["x"]).wait_recv()
+        self.k(1 - self.f, block).start()
+
+    def ready(self, f, block):
+        r = self.part(f, block, 1 - self.core)
+        remote(r, r, self.ks.at[f, block], self.kr.at[f, block], self.peers["core"]).wait_recv()
+
+    def finish(self):
+        c = self.c
+        for b in range(self.n):
+            self.x(b).wait_send()
+            self.k(1 - self.f, b).wait_send()
+            pl.when(c != b)(lambda b=b: self.k(self.f, b).wait_send())
+            pl.when((b >= c) & (c > 0))(lambda b=b: self.z(-1, b).wait_send())
+            pl.when((b <= c) & (c < self.n - 1))(lambda b=b: self.z(1, b).wait_send())
+
+
+class Home:
+    def __init__(self, refs, sems, where, width):
+        self.part, self.r1, self.mine, self.b2, self.r2, self.b3, self.r3, self.total = refs
+        self.send, self.recv = sems
+        self.f, self.c, self.t, self.core, self.peers = where
+        self.width = width
+
+    @staticmethod
+    def scratch(rows, width):
+        w = width // 2 + 128
+        return [
+            VM((2, 2, rows, w), BF),
+            VM((2, rows, w), BF),
+            VM((rows, w), F32),
+            VM((rows, w), BF),
+            VM((rows, w), BF),
+            VM((rows, w), BF),
+            VM((rows, w), BF),
+            VM((2, rows, width // 2), F32),
+        ]
+
+    def copy(self, i, src, dst, to):
+        return remote(src, dst, self.send.at[i], self.recv.at[i], self.peers[to])
+
+    def c1(self):
+        return self.copy(0, self.part.at[1 - self.core], self.r1, "core")
+
+    def c2(self):
+        return self.copy(1, self.b2, self.r2, "x")
+
+    def c3(self):
+        return self.copy(2, self.b3, self.r3, "y")
+
+    def c4(self):
+        r = self.total.at[self.core]
+        return self.copy(3, r, r, "core")
+
+    def s1(self):
+        self.c1().start()
+
+    def s2(self):
+        self.c1().wait_recv()
+        f, core = self.f, self.core
+        self.b2[...] = (self.part[core, 1 - f].astype(F32) + self.r1[1 - f].astype(F32)).astype(BF)
+        self.c2().start()
+        self.mine[...] = self.part[core, f].astype(F32) + self.r1[f].astype(F32)
+
+    def s3(self):
+        self.c2().wait_recv()
+        self.b3[...] = (self.mine[...] + self.r2[...].astype(F32)).astype(BF)
+        self.c3().start()
+
+    def s4(self):
+        self.c3().wait_recv()
+        whole = self.b3[...].astype(F32) + self.r3[...].astype(F32)
+        self.mine[...] = whole
+        self.total[self.core] = whole[:, : self.width // 2]
+        self.c4().start()
+
+    def s5(self):
+        self.c4().wait_recv()
+        for c in (self.c1, self.c2, self.c3, self.c4):
+            c().wait_send()
+
+
+def experts_kernel(
+    n_ctx, per, normed, cots, wexp, wrouter,
+    x_out, gh_out, dg_out, du_out, dn_out, ff_out, gg_out,
+    xs, gs, ws, gh, dg, du, own, wsem, gsem, osem, zs, zr, xsd, xr, ks, kr, *home,
+):
+    where = place()
+    f, c, t, core, peers = where
+    rows, width = normed.shape
+    half = width // 2
+    n_blk = 2 * n_ctx
+    loads = [
+        pltpu.make_async_copy(wexp.at[e, s], ws.at[s, :, pl.ds(e * 128, 128)], wsem)
+        for s in range(3) for e in range(per)
+    ]
+    for cp in loads:
+        cp.start()
+    gload = pltpu.make_async_copy(cots, gs, gsem)
+    gload.start()
+    xs[f * n_ctx + c] = normed[...]
+    greet(c, n_ctx, peers, f, t)
+    ga = Gather(xs, (zs, zr, xsd, xr, ks, kr), n_ctx, where)
+    ga.begin()
+    n_home = len(home) // 2
+    dnh = Home(home[: n_home - 2], home[n_home - 2 : n_home], where, width)
+    ffh = Home(home[n_home : 2 * n_home - 2], home[2 * n_home - 2 :], where, width)
+    lane = lax.broadcasted_iota(jnp.int32, (rows, 128), 1)
+
+    def block(ff, cc, keep):
+        b = ff * n_ctx + cc
+        xb, gb = xs[b], gs[b, :, :width]
+        lg = tdot(xb, wrouter[...], NN)
+        lg = jnp.where(lane < 2 * per, lg, -1e30)
+        ex = jnp.exp(lg - jnp.max(lg, -1, keepdims=True))
+        gates = ex / jnp.sum(ex, -1, keepdims=True)
+        gates = jnp.where(gs[b, :, width:].astype(F32) > 0.5, gates, 0.0)
+        gates = jnp.where(f == 0, gates[:, :per], gates[:, per : 2 * per])
+        gg = jnp.zeros((rows, 128), F32)
+        for p in range(per // 2):
+            cs = slice(p * 256, (p + 1) * 256)
+            gv = tdot(xb, ws[0, :, cs], NN)
+            uv = tdot(xb, ws[1, :, cs], NN)
+            bk = tdot(gb, ws[2, :, cs], NN)
+            ge = jnp.concatenate(
+                [jnp.broadcast_to(gates[:, e : e + 1], (rows, 128)) for e in (2 * p, 2 * p + 1)], 1
+            )
+            sig = 0.5 * jnp.tanh(0.5 * gv) + 0.5
+            act = gv * sig
+            hid = act * uv
+            dh = ge * bk
+            ghv = (ge * hid).astype(BF)
+            dgv = (dh * uv * (sig + act * (1.0 - sig))).astype(BF)
+            duv = (dh * act).astype(BF)
+            gh[b, :, cs] = ghv
+            dg[b, :, cs] = dgv
+            du[b, :, cs] = duv
+            if keep is not None:
+                own[0, keep, :, cs] = ghv
+                own[1, keep, :, cs] = dgv
+                own[2, keep, :, cs] = duv
+                hb = hid * bk
+                for i in range(2):
+                    s = jnp.sum(hb[:, i * 128 : (i + 1) * 128], -1, keepdims=True)
+                    gg = jnp.where(lane == f * per + 2 * p + i, s, gg)
+        for i, (src, dst) in enumerate(((gh, gh_out), (dg, dg_out), (du, du_out), (xs, x_out))):
+            pltpu.make_async_copy(src.at[b], dst.at[b], osem.at[i, b]).start()
+        return gg
+
+    def first(i, _):
+        ff = jnp.where(i == 0, f, 1 - f)
+
+        @pl.when(i == 1)
+        def _():
+            ga.cross(c)
+            ga.relay(1)
+            ga.ready(1 - f, c)
+
+        gg = block(ff, c, ff)
+        for h in range(2):
+            dnh.part[h, ff, :, half:] = gg.astype(BF)
+            ffh.part[h, ff, :, half:] = jnp.zeros((rows, 128), BF)
+        return 0
+
+    for cp in loads:
+        cp.wait()
+    gload.wait()
+    lax.fori_loop(0, 2, first, 0)
+
+    def dn_half(i, _):
+        h = jnp.where(i == 0, 1 - core, core)
+        rs = pl.ds(pl.multiple_of(h * half, 128), half)
+        v = tdot(own[1].reshape(2 * rows, per * 128), ws[0, rs, :], NT)
+        v = v + tdot(own[2].reshape(2 * rows, per * 128), ws[1, rs, :], NT)
+        dnh.part[h, :, :, :half] = v.astype(BF).reshape(2, rows, half)
+        pl.when(i == 0)(dnh.s1)
+        return 0
+
+    lax.fori_loop(0, 2, dn_half, 0)
+    dnh.s2()
+
+    def ff_half(i, _):
+        h = jnp.where(i == 0, 1 - core, core)
+        rs = pl.ds(pl.multiple_of(h * half, 128), half)
+        v = tdot(own[0].reshape(2 * rows, per * 128), ws[2, rs, :], NT)
+        ffh.part[h, :, :, :half] = v.astype(BF).reshape(2, rows, half)
+        pl.when(i == 0)(ffh.s1)
+        return 0
+
+    lax.fori_loop(0, 2, ff_half, 0)
+    ffh.s2()
+
+    for j in range(1, n_ctx):
+        cc = jnp.bitwise_xor(c, j)
+        if j > 1:
+            ga.relay(j)
+
+        def other(i, _):
+            ff = jnp.where(i == 0, f, 1 - f)
+            pl.when(i == 1)(lambda: ga.cross(cc))
+            ga.ready(ff, cc)
+            block(ff, cc, None)
+            return 0
+
+        lax.fori_loop(0, 2, other, 0)
+        if j == 1:
+            dnh.s3()
+        elif j == 2:
+            dnh.s4()
+            ffh.s3()
+    ffh.s4()
+    dnh.s5()
+    for h in range(2):
+        dn_out[:, h * half : (h + 1) * half] = dnh.total[h]
+    gg_out[...] = dnh.mine[:, half:]
+    ffh.s5()
+    for h in range(2):
+        ff_out[:, h * half : (h + 1) * half] = ffh.total[h]
+    ga.finish()
+    for b in range(n_blk):
+        for i, (src, dst) in enumerate(((gh, gh_out), (dg, dg_out), (du, du_out), (xs, x_out))):
+            pltpu.make_async_copy(src.at[b], dst.at[b], osem.at[i, b]).wait()
+
+
+def experts_call(normed, cots, wexp, wrouter, n_ctx):
+    rows, width = normed.shape
+    per = wexp.shape[0]
+    n_blk = 2 * n_ctx
+    hid = per * 128
+    anyspace = pl.BlockSpec(memory_space=pl.ANY)
+    vmem = pl.BlockSpec(memory_space=VM)
+    dma = pltpu.SemaphoreType.DMA
+    home = Home.scratch(rows, width) + [dma((4,)), dma((4,))]
+    shapes = [
+        ((n_blk, rows, width), BF),
+        ((n_blk, rows, hid), BF),
+        ((n_blk, rows, hid), BF),
+        ((n_blk, rows, hid), BF),
+        ((rows, width), F32),
+        ((rows, width), F32),
+        ((rows, 128), F32),
+    ]
+    return pl.pallas_call(
+        functools.partial(experts_kernel, n_ctx, per),
+        out_shape=[jax.ShapeDtypeStruct(s, d) for s, d in shapes],
+        in_specs=[vmem, anyspace, anyspace, vmem],
+        out_specs=[anyspace] * 4 + [vmem] * 3,
+        scratch_shapes=[
+            VM((n_blk, rows, width), BF),
+            VM((n_blk, rows, width + 128), BF),
+            VM((3, width, hid), BF),
+            VM((n_blk, rows, hid), BF),
+            VM((n_blk, rows, hid), BF),
+            VM((n_blk, rows, hid), BF),
+            VM((3, 2, rows, hid), BF),
+            dma, dma, dma((4, n_blk)),
+            *Gather.sems(n_ctx),
+            *home, *home,
+        ],
+        compiler_params=pltpu.CompilerParams(collective_id=2, has_side_effects=True, vmem_limit_bytes=62 << 20),
+        name="experts",
+    )(normed, cots, wexp, wrouter)
 
 
 def ancestry(parents):
@@ -66,7 +428,13 @@
 
     stream = residual_in[0].astype(F32)
     cot = out_cotangent[0]
-    cot_all = lax.all_gather(cot.astype(BF), ("fsdp", "context"), axis=0, tiled=True)
+    routes = expert_routes[0]
+    used = jnp.any(routes[:, :, None] == jnp.arange(experts, dtype=jnp.int32), 1)
+    fused = n_fs == 2 and n_ctx == 4
+    cot_low = cot.astype(BF)
+    if fused:
+        cot_low = jnp.concatenate([cot_low, jnp.pad(used.astype(BF), ((0, 0), (0, 128 - experts)))], 1)
+    cot_all = lax.all_gather(cot_low, ("fsdp", "context"), axis=0, tiled=True)
     gain_one = lax.all_gather(attn_gain, "fsdp", axis=0, tiled=True).astype(F32)
     gain_two = lax.all_gather(ffn_gain, "fsdp", axis=0, tiled=True).astype(F32)
     w_qkv = jnp.concatenate([query_weight, key_weight, value_weight], 1)
@@ -128,55 +496,73 @@
 
     logits = dot("ld,de->le", normed_two, w_router)
     router_probs = jax.nn.softmax(logits, -1)
-    routes = expert_routes[0]
-    used = jnp.any(routes[:, :, None] == jnp.arange(experts, dtype=jnp.int32), 1)
     gates = jnp.where(used, router_probs, 0.0)
 
-    normed_all = lax.all_gather(normed_two, ("fsdp", "context"), axis=0, tiled=True)
-    gates_all = lax.all_gather(gates, ("fsdp", "context"), axis=0, tiled=True)
-    gates_here = lax.dynamic_slice_in_dim(gates_all, fs * experts_here, experts_here, 1)
-    g3 = gates_here[:, :, None]
-    gate_val = dot("td,edf->tef", normed_all, expert_weights[:, 0])
-    up_val = dot("td,edf->tef", normed_all, expert_weights[:, 1])
-    back = dot("td,edf->tef", cot_all, expert_weights[:, 2])
-    sig = 1.0 / (1.0 + jnp.exp(-gate_val))
-    act = gate_val * sig
-    hid = act * up_val
-    gated_hid = (g3 * hid).astype(BF)
-    gate_grad_part = jnp.sum(hid * back, -1)
-    d_hid = g3 * back
-    d_gate_val = (d_hid * up_val * (sig * (1.0 + gate_val * (1.0 - sig)))).astype(BF)
-    d_up_val = (d_hid * act).astype(BF)
-
-    def own(z):
-        z = z.reshape((n_fs, n_ctx, rows) + z.shape[1:])
-        return lax.dynamic_index_in_dim(z, ctx, 1, keepdims=False)
-
-    ffn_part = dot("stef,edf->std", own(gated_hid), expert_weights[:, 2])
-    dn_part = dot("stef,edf->std", own(d_gate_val), expert_weights[:, 0]) + dot(
-        "stef,edf->std", own(d_up_val), expert_weights[:, 1]
-    )
-    gate_part = lax.dynamic_update_slice_in_dim(
-        jnp.zeros((n_fs, rows, experts), F32), own(gate_grad_part), fs * experts_here, 2
-    )
-
-    def home(z):
-        z = lax.psum_scatter(z.astype(BF), "fsdp", scatter_dimension=0, tiled=True)
-        return lax.psum(z, "tensor").astype(F32)[0]
-
-    dn = home(dn_part)
-    gate_grad = lax.psum(lax.psum_scatter(gate_part, "fsdp", scatter_dimension=0, tiled=True), "tensor")[0]
-    ffn_out = home(ffn_part)
-    block_out = middle + ffn_out
-
-    expert_grad = jnp.stack(
-        [
-            dot("td,tef->edf", normed_all, d_gate_val),
-            dot("td,tef->edf", normed_all, d_up_val),
-            dot("td,tef->edf", cot_all, gated_hid),
-        ],
-        1,
-    )
+    if fused:
+        x_all, gated_hid, d_gate_val, d_up_val, dn, ffn_out, gate_grad = experts_call(
+            normed_two, cot_all.reshape(n_fs * n_ctx, rows, -1), expert_weights,
+            jnp.pad(w_router, ((0, 0), (0, 128 - experts))), n_ctx
+        )
+        gate_grad = gate_grad[:, :experts]
+        block_out = middle + ffn_out
+        normed_all = x_all.reshape(-1, width)
+        gated_hid, d_gate_val, d_up_val = (
+            z.reshape(-1, experts_here, 128) for z in (gated_hid, d_gate_val, d_up_val)
+        )
+        expert_grad = jnp.stack(
+            [
+                dot("td,tef->edf", normed_all, d_gate_val),
+                dot("td,tef->edf", normed_all, d_up_val),
+                dot("td,tef->edf", cot_all[:, :width], gated_hid),
+            ],
+            1,
+        )
+    else:
+        normed_all = lax.all_gather(normed_two, ("fsdp", "context"), axis=0, tiled=True)
+        gates_all = lax.all_gather(gates, ("fsdp", "context"), axis=0, tiled=True)
+        gates_here = lax.dynamic_slice_in_dim(gates_all, fs * experts_here, experts_here, 1)
+        g3 = gates_here[:, :, None]
+        gate_val = dot("td,edf->tef", normed_all, expert_weights[:, 0])
+        up_val = dot("td,edf->tef", normed_all, expert_weights[:, 1])
+        back = dot("td,edf->tef", cot_all, expert_weights[:, 2])
+        sig = 1.0 / (1.0 + jnp.exp(-gate_val))
+        act = gate_val * sig
+        hid = act * up_val
+        gated_hid = (g3 * hid).astype(BF)
+        gate_grad_part = jnp.sum(hid * back, -1)
+        d_hid = g3 * back
+        d_gate_val = (d_hid * up_val * (sig * (1.0 + gate_val * (1.0 - sig)))).astype(BF)
+        d_up_val = (d_hid * act).astype(BF)
+
+        def own(z):
+            z = z.reshape((n_fs, n_ctx, rows) + z.shape[1:])
+            return lax.dynamic_index_in_dim(z, ctx, 1, keepdims=False)
+
+        ffn_part = dot("stef,edf->std", own(gated_hid), expert_weights[:, 2])
+        dn_part = dot("stef,edf->std", own(d_gate_val), expert_weights[:, 0]) + dot(
+            "stef,edf->std", own(d_up_val), expert_weights[:, 1]
+        )
+        gate_part = lax.dynamic_update_slice_in_dim(
+            jnp.zeros((n_fs, rows, experts), F32), own(gate_grad_part), fs * experts_here, 2
+        )
+
+        def home(z):
+            z = lax.psum_scatter(z.astype(BF), "fsdp", scatter_dimension=0, tiled=True)
+            return lax.psum(z, "tensor").astype(F32)[0]
+
+        dn = home(dn_part)
+        gate_grad = lax.psum(lax.psum_scatter(gate_part, "fsdp", scatter_dimension=0, tiled=True), "tensor")[0]
+        ffn_out = home(ffn_part)
+        block_out = middle + ffn_out
+
+        expert_grad = jnp.stack(
+            [
+                dot("td,tef->edf", normed_all, d_gate_val),
+                dot("td,tef->edf", normed_all, d_up_val),
+                dot("td,tef->edf", cot_all, gated_hid),
+            ],
+            1,
+        )
 
     own_mask = lax.dynamic_slice_in_dim(token_mask[0], ctx * rows, rows, 0).astype(F32)
     sums = [jnp.sum(jnp.sum(z * z, -1) * own_mask) for z in (stream, attn_out, middle, ffn_out)]

time: 665 us -> 516 us (0.78)
  waiting for transfers between devices: 334 us -> 197 us
  Pallas kernels: 0 us -> 79.9 us
  matrix products: 117 us -> 59 us
  blocking collectives: 114 us -> 72.6 us
  local copies, waits for them, and re-layouts: 34.8 us -> 44.8 us
    pallas_call x0 -> x1, Pallas kernels: none -> 79.9 us  [experts_call(): pl.pallas_call(functools.partial(experts_kernel, n_ctx, per), out_shape=[...]
    reduce_scatter x3 -> x0, waiting for transfers between devices: 58.2 us -> none  [the longest x2 45.8 us: home(): z = lax.psum_scatter(z.astype(BF), 'fsdp', scatter_dimension=0, tiled=True)]
    dot_general x24 -> x18, matrix products: 115 us -> 57.8 us  [dot(): return jnp.einsum(spec, a, b, preferred_element_type=F32)]
    all_gather x2 -> x1, waiting for transfers between devices: 114 us -> 69.3 us  [per_device(): cot_all = lax.all_gather(cot_low, ('fsdp', 'context'), axis=0, tiled=True)]
    psum x2 -> x1, waiting for transfers between devices: 42.7 us -> 0.02 us  [per_device(): lax.psum(dot('lc,dc->ld', d_qkv, w_qkv).astype(BF), 'tensor').astype(F32)]
    all_gather x1 -> x0, blocking collectives: 31.9 us -> none  [per_device(): gates_all = lax.all_gather(gates, ('fsdp', 'context'), axis=0, tiled=True)]
    psum x1 -> x0, blocking collectives: 11.7 us -> none  [per_device(): lax.psum(lax.psum_scatter(gate_part, 'fsdp', scatter_dimension=0, tiled=T...]
    reduce_scatter x1, waiting for transfers between devices: 15.5 us -> 24.7 us  [per_device(): lax.psum_scatter(dkv.astype(BF), 'context', scatter_dimension=0, tiled=True)]
  transfers between devices with their start and end apart: 15 -> 10, of which waited for: 14 -> 7; matrix products, arithmetic and copies ran while one was open for 19% -> 19% of each run, Pallas kernels for 0% -> 0%
where the time goes in v2:
time: 516 us; the launch traced here: 508 us
  waiting for transfers between devices  197 us (38%)
  Pallas kernels  79.9 us (15%)
  blocking collectives  72.6 us (14%)
  matrix products  59 us (11%)
  local copies, waits for them, and re-layouts  44.8 us (9%)
  other arithmetic  36.7 us (7%)
  between operations  17.3 us (3%)
    pallas_call x1, Pallas kernels, experts_call(): pl.pallas_call(functools.partial(experts_kernel, n_ctx, per), out_shape=[...  79.9 us
    all_gather x1, waiting for transfers between devices, per_device(): cot_all = lax.all_gather(cot_low, ('fsdp', 'context'), axis=0, tiled=True)  69.3 us
    dot_general x18, matrix products, dot(): return jnp.einsum(spec, a, b, preferred_element_type=F32)  57.8 us
    unnamed x129, local copies, waits for them, and re-layouts  32.8 us
    reduce_scatter x1, waiting for transfers between devices, per_device(): lax.psum_scatter(qkv_full.astype(BF), 'fsdp', scatter_dimension=0, tiled=...  32.8 us
    all_gather x1, waiting for transfers between devices, per_device(): w_qkv = lax.all_gather(w_qkv, 'fsdp', axis=0, tiled=True)  24.9 us
    reduce_scatter x1, waiting for transfers between devices, per_device(): lax.psum_scatter(dkv.astype(BF), 'context', scatter_dimension=0, tiled=True)  24.7 us
    psum x1, waiting for transfers between devices, per_device(): lax.psum(dot('lc,cd->ld', attended, w_out).astype(BF), 'tensor').astype(F32)  22.7 us
  transfers between devices with their start and end apart: 10, of which 7 were waited for; matrix products, arithmetic and copies ran while one was open for 19% of the time, Pallas kernels for 0%

profile of v2, /device:TPU:0, one launch (start us, length us, event | category | flops | bytes accessed | tf_op | source)
XLA Modules:
  0.0 507.7 jit_solution(12566905591211850131)
XLA Ops:
  11.3 5.2 %all-gather = bf16[2,1,768]{2,1,0:T(2,128)(2,1)S(1)} all-gather(bf16[1,1,768]{2,1,0:T(2,128)(2,1)S(1)} %reshape.254), channel_id=1, replica_groups=mesh['fsdp'=2,'context'=4,'tensor'=4] {'fsdp'}, dimensions={0}, use_global_device_ids=true | all-gather | bytes 4608 | tf_op jit(solution)/shard_map/all_gather | solution.py:438
  20.5 24.9 %all-gather.6.cloned.1.call-done = bf16[1536,640]{1,0:T(8,128)(2,1)} async-done(((bf16[768,640]{1,0:T(8,128)(2,1)}), bf16[1536,640]{1,0:T(8,128)(2,1)}) %all-gather.6.cloned.1.call-update) | async-done | bytes 1966096 | tf_op jit(solution)/shard_map/all_gather | solution.py:441
  48.1 15.6 %all_gather.23 = bf16[1024,256]{1,0:T(8,128)(2,1)S(1)} all-gather(bf16[256,256]{1,0:T(8,128)(2,1)S(1)} %pad_maximum_fusion.8), channel_id=1, replica_groups=mesh['fsdp'=2,'context'=4,'tensor'=4] {'context'}, dimensions={0}, use_global_device_ids=true | all-gather | bytes 655360 | tf_op jit(solution)/shard_map/all_gather | solution.py:481
  74.1 4.3 all-gather.1
  78.7 6.3 %all_gather.27 = bf16[1536,16]{1,0:T(8,128)(2,1)S(1)} all-gather(bf16[768,16]{1,0:T(8,128)(2,1)S(1)} %copy.97), channel_id=1, replica_groups=mesh['fsdp'=2,'context'=4,'tensor'=4] {'fsdp'}, dimensions={0}, use_global_device_ids=true | all-gather | bytes 73728 | tf_op jit(solution)/shard_map/all_gather | solution.py:443
  85.8 22.7 %all-reduce.7.cloned.1.call-done = bf16[256,1536]{1,0:T(8,128)(2,1)} async-done(((bf16[256,1536]{1,0:T(8,128)(2,1)}), bf16[256,1536]{1,0:T(8,128)(2,1)}) %all-reduce.7.cloned.1.call-update) | async-done | bytes 786448 | tf_op jit(solution)/shard_map/psum | solution.py:492
  112.6 69.3 %all-gather.10.cloned.1.call-done = bf16[2048,1664]{1,0:T(8,128)(2,1)} async-done(((bf16[256,1664]{1,0:T(8,128)(2,1)}), bf16[2048,1664]{1,0:T(8,128)(2,1)}) %all-gather.10.cloned.1.call-update) | async-done | bytes 6815760 | tf_op jit(solution)/shard_map/all_gather | solution.py:437
  181.9 79.9 %experts.1 = (bf16[8,256,1536]{2,1,0:T(8,128)(2,1)}, bf16[8,256,1024]{2,1,0:T(8,128)(2,1)}, bf16[8,256,1024]{2,1,0:T(8,128)(2,1)}, bf16[8,256,1024]{2,1,0:T(8,12...) custom-call(bf16[256,1536]{1,0:T(8,128)(2,1)} %copy-done.7, ...), custom_call_target="tpu_custom_call" | custom-call | tf_op jit(solution)/shard_map/experts/pallas_call | solution.py:353
  263.0 3.3 multiply_reduce_fusion.1
  272.5 5.4 %fusion.24 = bf16[2,64,1024]{2,1,0:T(8,128)(2,1)} fusion(bf16[256,2,3,64]{0,3,2,1:T(8,128)(2,1)} %bitcast.197, f32[2,1024,256,3]{2,1,3,0:T(8,128)} %copy-done, f32[2,3,256]{2,1,0:T(4,128)S(1)} %log_add_fusion, pred[256,1024]{0,1:T(8,128)(4,1)S(1)} %fusion.26), kind=kOutput, calls=%fused_computation.56 | convolution fusion | flops 207749120 | bytes 7018496 | tf_op jit(solution)/shard_map/kglm,lkgh->mkh/dot_general | solution.py:386
  288.0 24.7 %reduce-scatter.5.cloned.1.call-done = bf16[256,256]{0,1:T(8,128)(2,1)} async-done(((bf16[1024,256]{0,1:T(8,128)(2,1)}), bf16[256,256]{0,1:T(8,128)(2,1)}) %reduce-scatter.5.cloned.1.call-update) | async-done | bytes 131088 | tf_op jit(solution)/shard_map/reduce_scatter | solution.py:588
  314.5 3.4 convolution_convert_fusion.2
  323.2 3.5 copy.118
  331.3 8.9 %convolution_bitcast_fusion = f32[8,1,1536,128]{2,3,0,1:T(8,128)} fusion(bf16[2048,1536,1]{1,0,2:T(8,128)(2,1)S(1)} %bitcast.209, bf16[2048,8,128]{2,1,0:T(8,128)(2,1)S(1)} %bitcast.184), kind=kOutput, calls=%fused_computation.13 | convolution fusion | flops 6442450944 | bytes 16777216 | tf_op jit(solution)/shard_map/td,tef->edf/dot_general | solution.py:386
  340.2 8.8 %convolution_bitcast_fusion.1 = f32[8,1,1536,128]{2,3,0,1:T(8,128)} fusion(bf16[2048,1536,1]{1,0,2:T(8,128)(2,1)S(1)} %bitcast.210, bf16[2048,8,128]{2,1,0:T(8,128)(2,1)S(1)} %bitcast.183), kind=kOutput, calls=%fused_computation.14 | convolution fusion | flops 6442450944 | bytes 16777216 | tf_op jit(solution)/shard_map/td,tef->edf/dot_general | solution.py:386
  349.0 8.8 %fusion.5 = f32[8,1,1536,128]{2,3,0,1:T(8,128)} fusion(bf16[2048,1664]{1,0:T(8,128)(2,1)S(1)} %bitcast.178, bf16[2048,8,128]{2,1,0:T(8,128)(2,1)S(1)} %bitcast.182), kind=kOutput, calls=%fused_computation.12 | convolution fusion | flops 6442450944 | bytes 16777216 | tf_op jit(solution)/shard_map/td,tef->edf/dot_general | solution.py:386
  360.9 3.3 stack.39
  364.2 11.3 %reduce-scatter.11.cloned.1.call-done = bf16[384,768]{1,0:T(8,128)(2,1)} async-done(((bf16[384,1536]{1,0:T(8,128)(2,1)}), bf16[384,768]{1,0:T(8,128)(2,1)}) %reduce-scatter.11.cloned.1.call-update) | async-done | bytes 589840 | tf_op jit(solution)/shard_map/reduce_scatter | solution.py:598
  375.5 32.8 %reduce-scatter.9.cloned.1.call-done = bf16[768,640]{1,0:T(8,128)(2,1)} async-done(((bf16[1536,640]{1,0:T(8,128)(2,1)}), bf16[768,640]{1,0:T(8,128)(2,1)}) %reduce-scatter.9.cloned.1.call-update) | async-done | bytes 983056 | tf_op jit(solution)/shard_map/reduce_scatter | solution.py:597
  408.3 12.9 %pad_maximum_fusion = f32[8,3,1536,128]{2,3,0,1:T(8,128)} fusion(f32[8,1,1536,128]{2,3,0,1:T(8,128)} %fusion.5, f32[8,1,1536,128]{2,3,0,1:T(8,128)} %convolution_bitcast_fusion, f32[8,1,1536,128]{2,3,0,1:T(8,128)} %convolution_bitcast_fusion.1), kind=kLoop, calls=%fused_computation | loop fusion | flops 9437184 | bytes 37748736 | tf_op jit(solution)/shard_map/stack | solution.py:512
  421.1 21.1 %psum.47 = f32[5]{0:T(128)S(1)} all-reduce(f32[5]{0:T(128)S(1)} %stack.39), channel_id=1, replica_groups=mesh['fsdp'=2,'context'=4,'tensor'=4] {'fsdp','context'}, use_global_device_ids=true, to_apply=%region_30.31 | all-reduce | flops 5 | bytes 40 | tf_op jit(solution)/shard_map/psum | solution.py:569
  442.3 18.7 %copy.107 = f32[8,3,1536,128]{3,2,1,0:T(8,128)} copy(f32[8,3,1536,128]{2,3,0,1:T(8,128)} %pad_maximum_fusion) | data formatting | bytes 37748736
  464.4 20.0 %psum.44 = f32[768,18]{0,1:T(8,128)S(1)} all-reduce(f32[768,18]{0,1:T(8,128)} %reduce-scatter.7.cloned.1.call-done), channel_id=1, replica_groups=mesh['fsdp'=2,'context'=4,'tensor'=4] {'context'}, use_global_device_ids=true, to_apply=%region_18.19 | all-reduce | flops 13824 | bytes 110592 | tf_op jit(solution)/shard_map/psum | solution.py:600
  485.6 10.3 %all-reduce.11.cloned.1.call-done = (bf16[768,640]{1,0:T(8,128)(2,1)}, bf16[384,768]{1,0:T(8,128)(2,1)}) async-done(((bf16[768,640]{1,0:T(8,128)(2,1)}, bf16[384,768]{1,0:T(8,128)(2,1)}), (bf16[768,640]{1,0:T(8,128)(2,1)}, bf16[384,768]{1,0:T(8,128)(2,1)})) %all-reduce.11.cloned.1.call-update) | async-done | bytes 1572880 | tf_op jit(solution)/shard_map/psum | solution.py:597
  (241 shorter events, 64.9 us)
Async XLA Ops:
  8.0 8.6 %copy-start.1 = (bf16[1,256,1536]{2,1,0:T(8,128)(2,1)S(1)}, bf16[1,256,1536]{2,1,0:T(8,128)(2,1)}, u32[]{:S(2)}) copy-start(bf16[1,256,1536]{2,1,0:T(8,128)(2,1)} %param.13) | copy-start | bytes 2359300
  8.0 9.4 %copy-start.54 = (s32[1,8]{1,0:T(1,128)S(1)}, s32[1,8]{1,0:T(1,128)}, u32[]{:S(2)}) copy-start(s32[1,8]{1,0:T(1,128)} %param.15) | copy-start | bytes 100
  8.0 37.3 %all-gather.6.cloned.1.call-start = ((), (), s32[]{:S(2)}) async-start(), calls=%async_computation.4 | async-start | bytes 2949120 | tf_op jit(solution)/shard_map/all_gather | solution.py:441
  10.5 8.4 %copy-start.47 = (s32[1,1024]{1,0:T(1,128)S(1)}, s32[1,1024]{1,0:T(1,128)}, u32[]{:S(2)}) copy-start(s32[1,1024]{1,0:T(1,128)} %param.14) | copy-start | bytes 12292
  10.5 8.8 %copy-start.9 = (f32[1,256,1536]{2,1,0:T(8,128)S(1)}, f32[1,256,1536]{2,1,0:T(8,128)}, u32[]{:S(2)}) copy-start(f32[1,256,1536]{2,1,0:T(8,128)} %param.25) | copy-start | bytes 4718596
  10.5 59.4 %all-gather.8.cloned.1.call-start = ((), (), s32[]{:S(2)}) async-start(), calls=%async_computation.5 | async-start | bytes 1769472 | tf_op jit(solution)/shard_map/all_gather | solution.py:442
  11.2 97.3 %all-reduce.7.cloned.1.call-start = ((), (), s32[]{:S(2)}) async-start(), calls=%async_computation.6 | async-start | bytes 1572864 | tf_op jit(solution)/shard_map/psum | solution.py:492
  16.9 30.9 %copy-start.38 = (f32[256]{0:T(256)}, f32[256]{0:T(256)S(1)}, u32[]{:S(2)}) copy-start(f32[256]{0:T(256)S(1)} %add_rsqrt_fusion.1) | copy-start | bytes 3076
  18.8 45.6 %copy-start.19 = (f32[256,64]{0,1:T(8,128)}, f32[256,64]{0,1:T(8,128)S(1)}, u32[]{:S(2)}) copy-start(f32[256,64]{0,1:T(8,128)S(1)} %get-tuple-element.101) | copy-start | bytes 196612
  18.8 45.6 %copy-start.21 = (f32[256,64]{0,1:T(8,128)}, f32[256,64]{0,1:T(8,128)S(1)}, u32[]{:S(2)}) copy-start(f32[256,64]{0,1:T(8,128)S(1)} %get-tuple-element.102) | copy-start | bytes 196612
  72.8 109.1 %all-gather.10.cloned.1.call-start = ((), (), s32[]{:S(2)}) async-start(), calls=%async_computation.7 | async-start | bytes 7667712 | tf_op jit(solution)/shard_map/all_gather | solution.py:437
  73.0 190.0 %copy-start.30 = (pred[256,16]{1,0:T(32,128)(4,1)}, pred[256,16]{1,0:T(32,128)(4,1)S(1)}, u32[]{:S(2)}) copy-start(pred[256,16]{1,0:T(32,128)(4,1)S(1)} %copy.96) | copy-start | bytes 12292
  74.0 238.7 %reduce-scatter.5.cloned.1.call-start = ((), (), s32[]{:S(2)}) async-start(), calls=%async_computation.8 | async-start | bytes 655360 | tf_op jit(solution)/shard_map/reduce_scatter | solution.py:588
  112.3 150.7 %copy-start.36 = (f32[256]{0:T(256)}, f32[256]{0:T(256)S(1)}, u32[]{:S(2)}) copy-start(f32[256]{0:T(256)S(1)} %get-tuple-element.110) | copy-start | bytes 3076
  112.5 150.5 %copy-start.44 = (f32[256]{0:T(256)}, f32[256]{0:T(256)S(1)}, u32[]{:S(2)}) copy-start(f32[256]{0:T(256)S(1)} %fusion.41) | copy-start | bytes 3076
  269.5 8.4 %slice-start = ((s8[6291456]{0:T(1024)(128)(4,1)}), s8[2097152]{0:T(1024)(128)(4,1)S(1)}, s32[]{:S(2)}) async-start(s8[6291456]{0:T(1024)(128)(4,1)} %bitcast.174), calls=%async_computation.14 | async-start | bytes 4194304
  285.2 72.6 %all-reduce.9.cloned.1.call-start = ((), (), s32[]{:S(2)}) async-start(), calls=%async_computation.9 | async-start | bytes 1572864 | tf_op jit(solution)/shard_map/psum | solution.py:593
  318.0 57.5 %reduce-scatter.11.cloned.1.call-start = ((), (), s32[]{:S(2)}) async-start(), calls=%async_computation.12 | async-start | bytes 1769472 | tf_op jit(solution)/shard_map/reduce_scatter | solution.py:598
  319.6 88.7 %reduce-scatter.9.cloned.1.call-start = ((), (), s32[]{:S(2)}) async-start(), calls=%async_computation.11 | async-start | bytes 2949120 | tf_op jit(solution)/shard_map/reduce_scatter | solution.py:597
  321.8 142.5 %reduce-scatter.7.cloned.1.call-start = ((), (), s32[]{:S(2)}) async-start(), calls=%async_computation.10 | async-start | bytes 221184 | tf_op jit(solution)/shard_map/reduce_scatter | solution.py:600
  331.3 17.7 %slice-start.2 = ((s8[6815744]{0:T(1024)(128)(4,1)}), s8[4194304]{0:T(1024)(128)(4,1)S(1)}, s32[]{:S(2)}) async-start(s8[6815744]{0:T(1024)(128)(4,1)} %bitcast.177), calls=%async_computation.16 | async-start | bytes 8388608
  340.2 8.8 %slice-start.3 = ((s8[6815744]{0:T(1024)(128)(4,1)}), s8[2621440]{0:T(1024)(128)(4,1)S(1)}, s32[]{:S(2)}) async-start(s8[6815744]{0:T(1024)(128)(4,1)} %bitcast.177), calls=%async_computation.17 | async-start | bytes 5242880
  360.2 135.7 %all-reduce.11.cloned.1.call-start = ((), (), s32[]{:S(2)}) async-start(), calls=%async_computation.13 | async-start | bytes 3145728 | tf_op jit(solution)/shard_map/psum | solution.py:597
  442.3 20.5 %copy-start.15 = (bf16[256,1536]{1,0:T(8,128)(2,1)S(1)}, bf16[256,1536]{1,0:T(8,128)(2,1)}, u32[]{:S(2)}) copy-start(bf16[256,1536]{1,0:T(8,128)(2,1)} %all-reduce.9.cloned.1.call-done) | copy-start | bytes 2359300
  (47 other events, 125.3 us)
Sparse Core Ops, SparseCore 0:
  11.0 34.3 all-gather.5
  46.9 22.7 all-gather.7
  72.9 35.5 all-reduce.6
  285.3 27.3 reduce-scatter.4
  318.1 32.8 all-reduce.8
  353.7 21.7 reduce-scatter.10
  377.8 30.3 reduce-scatter.8
  411.0 10.4 reduce-scatter.6
  424.0 71.9 all-reduce.10
Sparse Core Ops, SparseCore 1:
  76.0 105.9 all-gather.9
